TPU v7x, 1024 devices: a whole 4x4x32 slice. The times are simulated.
1024 devices in a mesh: band: 128 (over x, z), sub: 8 (over y, core).
Axes of the slice: x: 4, y: 4, z: 32, core: 2. Of those that a mesh axis runs over, the one named last changes fastest.
Arguments:
- atmos_flux: bfloat16 [32, 1024, 1024], P(None, 'band', 'sub'), may hold values from -6 to 6
- weight_tiles: bfloat16 [128, 8, 32, 384, 128], P('band', 'sub'), may hold values from -0.3125 to 0.3125
- source_row: int32 [128, 8, 32], P('band', 'sub'), may hold values from 0 to 7
- target_code: int32 [128, 8, 32], P('band', 'sub'), may hold values from 0 to 127
- live_count: int32 [128, 8], P('band', 'sub'), may hold values from 8 to 32, as said below
Outputs:
- ocean_flux: float32 [32, 1048576], P(None, ('band', 'sub'))
Inputs may be any that keep to these rules, and one draw needn't show every extreme that they name: `live_count`: each device has between 8 and 32 live entries; some device has exactly 32.
All inputs are finite; a program needn't handle non-finite values.
Results may differ from a plain program's by a relative error of at most 0.0036.
Values may be sent and summed in bfloat16 or wider, within the bound.
No kernel may reach another device: no remote copies, remote signals or barrier semaphores. Data moves between devices by JAX's collectives and lax.ppermute only.
A program may use at most 32 MiB of HBM per device.

v0:
```python
import jax
import jax.numpy as jnp
from jax import lax
from jax.sharding import PartitionSpec as P

OB_DEV = 8


def with_halo(x, sides, width):
    for axis, dim in sides:
        count, length = (lax.axis_size(axis), x.shape[dim])
        up = [(i, (i + 1) % count) for i in range(count - 1)]
        down = [(j, i) for i, j in up]
        last = lax.slice_in_dim(x, length - width, length, axis=dim)
        leading = lax.slice_in_dim(x, 0, width, axis=dim)
        before = lax.ppermute(last, axis, up)
        after = lax.ppermute(leading, axis, down)
        x = jnp.concatenate([before, x, after], axis=dim)
    return x


def passed_along(value, axis, steps):
    count = lax.axis_size(axis)
    pairs = [(source, (source + steps) % count) for source in range(count)]
    return lax.ppermute(value, axis, pairs)


def shards(atmos_flux, weight_tiles, source_row, target_code, live_count):
    fields = atmos_flux.shape[0]
    width = atmos_flux.shape[2]
    capacity = weight_tiles.shape[2]
    subs = lax.axis_size("sub")
    owned = OB_DEV
    widened = with_halo(atmos_flux, (("band", 1), ("sub", 2)), 1)
    wide_float = widened.astype(jnp.float32)
    grad_x = (0.5 * (wide_float[:, 1:-1, 2:] - wide_float[:, 1:-1, :-2])).astype(jnp.bfloat16)
    grad_y = (0.5 * (wide_float[:, 2:, 1:-1] - wide_float[:, :-2, 1:-1])).astype(jnp.bfloat16)
    operand = jnp.concatenate([atmos_flux, grad_x, grad_y], axis=-1).transpose(1, 0, 2)
    picked = operand[source_row[0, 0]]
    product = jnp.einsum(
        "ekc,ecl->ekl", picked, weight_tiles[0, 0], preferred_element_type=jnp.float32
    )
    targets = 2 * subs * owned
    live = (jnp.arange(capacity, dtype=jnp.int32) < live_count[0, 0]).astype(jnp.float32)
    selector = (target_code[0, 0][None, :] == jnp.arange(targets, dtype=jnp.int32)[:, None]).astype(
        jnp.float32
    ) * live[None, :]
    summed = jnp.einsum("te,ekl->tkl", selector, product, precision=lax.Precision.HIGHEST)
    outgoing = summed.astype(jnp.bfloat16).reshape(subs, 2, owned, fields, width)
    received = lax.all_to_all(outgoing, "sub", split_axis=0, concat_axis=0, tiled=True)
    own_band = jnp.sum(received[:, 0].astype(jnp.float32), axis=0)
    arrived = passed_along(received[:, 1], "band", 1)
    next_band = jnp.sum(arrived.astype(jnp.float32), axis=0)
    total = own_band + next_band
    return total.transpose(1, 0, 2).reshape(fields, owned * width)


def solution(mesh):
    return jax.shard_map(
        shards,
        mesh=mesh,
        in_specs=(
            P(None, "band", "sub"),
            P("band", "sub", None, None, None),
            P("band", "sub", None),
            P("band", "sub", None),
            P("band", "sub"),
        ),
        out_specs=P(None, ("band", "sub")),
        check_vma=False,
    )
```

profile of v0, /device:TPU:6, one launch (start us, length us, event | category | flops | bytes accessed | tf_op | source)
XLA Modules:
  0.0 81.7 jit_solution(14671788226004972722)
XLA Ops:
  0.0 0.0 copy-start
  0.0 1.0 %copy.13 = bf16[32,8,128]{2,0,1:T(8,128)(2,1)S(1)} copy(bf16[32,8,128]{2,1,0:T(8,128)(2,1)} %param.5) | data formatting | bytes 131072 | tf_op args[0]
  1.0 18.9 %collective-permute-start.1 = (bf16[32,1,128]{2,0,1:T(8,128)(2,1)S(1)}, bf16[32,1,128]{2,0,1:T(8,128)(2,1)S(1)}, u32[]{:S(2)}, u32[]{:S(2)}) collective-permute-start(bf16[32,1,128]{2,0,1:T(8,128)(2,1)S(1)} %get-tuple-element.9), channel_id=1, source_target_pairs={{8,0},{16,8},{24,16},{32,24},{40,32},{48,40},{56,48},{64,56},{72,6... | collective-permute-start | bytes 24584 | tf_op jit(solution)/shard_map/ppermute | solution.py:17
  20.0 1.9 %collective-permute-start = (bf16[32,1,128]{2,0,1:T(8,128)(2,1)S(1)}, bf16[32,1,128]{2,0,1:T(8,128)(2,1)S(1)}, u32[]{:S(2)}, u32[]{:S(2)}) collective-permute-start(bf16[32,1,128]{2,0,1:T(8,128)(2,1)S(1)} %get-tuple-element.10), channel_id=1, source_target_pairs={{0,8},{8,16},{16,24},{24,32},{32,40},{40,48},{48,56},{56,64},{64,7... | collective-permute-start | bytes 24584 | tf_op jit(solution)/shard_map/ppermute | solution.py:16
  21.9 0.7 fusion.12
  23.2 4.4 %collective-permute-done = bf16[32,1,128]{2,0,1:T(8,128)(2,1)S(1)} collective-permute-done((bf16[32,1,128]{2,0,1:T(8,128)(2,1)S(1)}, bf16[32,1,128]{2,0,1:T(8,128)(2,1)S(1)}, u32[]{:S(2)}, u32[]{:S(2)}) %collective-permute-start) | collective-permute-done | bytes 8224 | tf_op jit(solution)/shard_map/ppermute | solution.py:16
  27.6 0.9 %constant_dynamic-update-slice_fusion.1 = bf16[32,10,128]{2,0,1:T(8,128)(2,1)S(1)} fusion(bf16[32,10,128]{2,0,1:T(8,128)(2,1)S(1)} %constant_dynamic-update-slice_fusion.2, bf16[32,8,128]{2,1,0:T(8,128)(2,1)} %param.5), kind=kLoop, calls=%fused_computation.24 | loop fusion | bytes 131072
  28.5 0.0 collective-permute-done.1
  28.5 0.1 fusion.14
  28.6 1.3 %collective-permute-start.2 = (bf16[32,10,1]{2,0,1:T(8,128)(2,1)S(1)}, bf16[32,10,1]{2,0,1:T(8,128)(2,1)S(1)}, u32[]{:S(2)}, u32[]{:S(2)}) collective-permute-start(bf16[32,10,1]{2,0,1:T(8,128)(2,1)S(1)} %get-tuple-element.7), channel_id=1, source_target_pairs={{0,1},{1,2},{2,3},{3,4},{4,5},{5,6},{6,7},{8,9},{9,10},{10,11},{11... | collective-permute-start | bytes 1928 | tf_op jit(solution)/shard_map/ppermute | solution.py:16
  29.9 1.3 %collective-permute-start.3 = (bf16[32,10,1]{2,0,1:T(8,128)(2,1)S(1)}, bf16[32,10,1]{2,0,1:T(8,128)(2,1)S(1)}, u32[]{:S(2)}, u32[]{:S(2)}) collective-permute-start(bf16[32,10,1]{2,0,1:T(8,128)(2,1)S(1)} %get-tuple-element.8), channel_id=1, source_target_pairs={{1,0},{2,1},{3,2},{4,3},{5,4},{6,5},{7,6},{9,8},{10,9},{11,10},{12... | collective-permute-start | bytes 1928 | tf_op jit(solution)/shard_map/ppermute | solution.py:17
  31.2 0.0 collective-permute-done.2
  31.2 3.7 %collective-permute-done.3 = bf16[32,10,1]{2,0,1:T(8,128)(2,1)S(1)} collective-permute-done((bf16[32,10,1]{2,0,1:T(8,128)(2,1)S(1)}, bf16[32,10,1]{2,0,1:T(8,128)(2,1)S(1)}, u32[]{:S(2)}, u32[]{:S(2)}) %collective-permute-start.3) | collective-permute-done | bytes 672 | tf_op jit(solution)/shard_map/ppermute | solution.py:17
  34.9 0.1 maximum_convert_fusion
  35.0 0.2 fusion.6
  35.2 0.0 copy-start.1
  35.3 1.5 %gather_fusion = bf16[32,32,384]{2,1,0:T(8,128)(2,1)} fusion(bf16[8,32,384]{2,1,0:T(8,128)(2,1)S(1)} %maximum_bitcast_fusion, s32[1024]{0:T(1024)S(1)} %pad_clamp_fusion), kind=kCustom, calls=%fused_computation | custom fusion | bytes 1572992 | tf_op jit(solution)/shard_map/gather | solution.py:39
  36.8 0.0 copy-done
  36.8 1.8 %fusion = f32[32,32,128]{2,1,0:T(8,128)S(1)} fusion(bf16[32,32,384]{2,1,0:T(8,128)(2,1)} %gather_fusion, bf16[1,1,32,384,128]{4,3,2,1,0:T(8,128)(2,1)S(1)} %copy-done), kind=kOutput, calls=%fused_computation.1 | convolution fusion | flops 100663296 | bytes 4456448 | tf_op jit(solution)/shard_map/ekc,ecl->ekl/dot_general | solution.py:40
  38.6 0.0 copy-done.1
  38.6 1.9 %convolution_convert_fusion = bf16[128,32,128]{2,0,1:T(8,128)(2,1)S(1)} fusion(f32[32,32,128]{2,1,0:T(8,128)S(1)} %fusion, f32[32]{0:T(128)S(1)} %compare_convert_fusion, s32[32]{0:T(128)S(1)} %bitcast.26), kind=kOutput, calls=%fused_computation.3 | convolution fusion | flops 201859072 | bytes 1573120 | tf_op jit(solution)/shard_map/te,ekl->tkl/dot_general | solution.py:48
  40.5 0.2 copy.15
  40.7 22.8 %all_to_all.5 = bf16[8,2,8,32,128]{4,2,1,3,0:T(8,128)(2,1)S(1)} all-to-all(bf16[8,2,8,32,128]{4,2,1,3,0:T(8,128)(2,1)S(1)} %copy.15), channel_id=1, replica_groups=mesh['band'=128,'sub'=8] {'sub'}, dimensions={0} | all-to-all | bytes 2097152 | tf_op jit(solution)/shard_map/all_to_all | solution.py:50
  63.5 0.1 slice_bitcast_fusion
  63.6 1.9 %collective-permute-start.4 = (bf16[8,8,32,128]{3,1,2,0:T(8,128)(2,1)S(1)}, bf16[8,8,32,128]{3,1,2,0:T(8,128)(2,1)S(1)}, u32[]{:S(2)}, u32[]{:S(2)}) collective-permute-start(bf16[8,8,32,128]{3,1,2,0:T(8,128)(2,1)S(1)} %slice_bitcast_fusion), channel_id=1, source_target_pairs={{0,8},{8,16},{16,24},{24,32},{32,40},{40,48},{48,56},{56,64},{64,7... | collective-permute-start | bytes 1572872 | tf_op jit(solution)/shard_map/ppermute | solution.py:25
  65.5 0.1 convert_reduce_fusion.1
  65.6 15.3 %collective-permute-done.4 = bf16[8,8,32,128]{3,1,2,0:T(8,128)(2,1)S(1)} collective-permute-done((bf16[8,8,32,128]{3,1,2,0:T(8,128)(2,1)S(1)}, bf16[8,8,32,128]{3,1,2,0:T(8,128)(2,1)S(1)}, u32[]{:S(2)}, u32[]{:S(2)}) %collective-permute-start.4) | collective-permute-done | bytes 524320 | tf_op jit(solution)/shard_map/ppermute | solution.py:25
  80.9 0.1 convert_reduce_fusion
  81.0 0.7 copy.21
  (7 shorter events, 0.1 us)
Async XLA Ops:
  0.0 36.8 %copy-start = (bf16[1,1,32,384,128]{4,3,2,1,0:T(8,128)(2,1)S(1)}, bf16[1,1,32,384,128]{4,3,2,1,0:T(8,128)(2,1)}, u32[]{:S(2)}) copy-start(bf16[1,1,32,384,128]{4,3,2,1,0:T(8,128)(2,1)} %param.6) | copy-start | bytes 9437188
  1.0 27.5 %collective-permute-start.1 = (bf16[32,1,128]{2,0,1:T(8,128)(2,1)S(1)}, bf16[32,1,128]{2,0,1:T(8,128)(2,1)S(1)}, u32[]{:S(2)}, u32[]{:S(2)}) collective-permute-start(bf16[32,1,128]{2,0,1:T(8,128)(2,1)S(1)} %get-tuple-element.9), channel_id=1, source_target_pairs={{8,0},{16,8},{24,16},{32,24},{40,32},{48,40},{56,48},{64,56},{72,6... | collective-permute-start | bytes 24584 | tf_op jit(solution)/shard_map/ppermute | solution.py:17
  20.0 7.7 %collective-permute-start = (bf16[32,1,128]{2,0,1:T(8,128)(2,1)S(1)}, bf16[32,1,128]{2,0,1:T(8,128)(2,1)S(1)}, u32[]{:S(2)}, u32[]{:S(2)}) collective-permute-start(bf16[32,1,128]{2,0,1:T(8,128)(2,1)S(1)} %get-tuple-element.10), channel_id=1, source_target_pairs={{0,8},{8,16},{16,24},{24,32},{32,40},{40,48},{48,56},{56,64},{64,7... | collective-permute-start | bytes 24584 | tf_op jit(solution)/shard_map/ppermute | solution.py:16
  28.6 2.6 %collective-permute-start.2 = (bf16[32,10,1]{2,0,1:T(8,128)(2,1)S(1)}, bf16[32,10,1]{2,0,1:T(8,128)(2,1)S(1)}, u32[]{:S(2)}, u32[]{:S(2)}) collective-permute-start(bf16[32,10,1]{2,0,1:T(8,128)(2,1)S(1)} %get-tuple-element.7), channel_id=1, source_target_pairs={{0,1},{1,2},{2,3},{3,4},{4,5},{5,6},{6,7},{8,9},{9,10},{10,11},{11... | collective-permute-start | bytes 1928 | tf_op jit(solution)/shard_map/ppermute | solution.py:16
  29.9 5.0 %collective-permute-start.3 = (bf16[32,10,1]{2,0,1:T(8,128)(2,1)S(1)}, bf16[32,10,1]{2,0,1:T(8,128)(2,1)S(1)}, u32[]{:S(2)}, u32[]{:S(2)}) collective-permute-start(bf16[32,10,1]{2,0,1:T(8,128)(2,1)S(1)} %get-tuple-element.8), channel_id=1, source_target_pairs={{1,0},{2,1},{3,2},{4,3},{5,4},{6,5},{7,6},{9,8},{10,9},{11,10},{12... | collective-permute-start | bytes 1928 | tf_op jit(solution)/shard_map/ppermute | solution.py:17
  35.2 3.4 %copy-start.1 = (s32[1,1,32]{2,1,0:T(1,128)S(1)}, s32[1,1,32]{2,1,0:T(1,128)}, u32[]{:S(2)}) copy-start(s32[1,1,32]{2,1,0:T(1,128)} %param.8) | copy-start | bytes 388
  63.6 17.3 %collective-permute-start.4 = (bf16[8,8,32,128]{3,1,2,0:T(8,128)(2,1)S(1)}, bf16[8,8,32,128]{3,1,2,0:T(8,128)(2,1)S(1)}, u32[]{:S(2)}, u32[]{:S(2)}) collective-permute-start(bf16[8,8,32,128]{3,1,2,0:T(8,128)(2,1)S(1)} %slice_bitcast_fusion), channel_id=1, source_target_pairs={{0,8},{8,16},{16,24},{24,32},{32,40},{40,48},{48,56},{56,64},{64,7... | collective-permute-start | bytes 1572872 | tf_op jit(solution)/shard_map/ppermute | solution.py:25
where the time goes:
time: 82 us; the launch traced here: 81.7 us
  starting transfers between devices  25.4 us (31%)
  waiting for transfers between devices  23.4 us (29%)
  blocking collectives  22.8 us (28%)
  local copies, waits for them, and re-layouts  4.48 us (5%)
  matrix products  3.71 us (5%)
  other arithmetic  1.16 us (1%)
    all_to_all x1, blocking collectives, shards(): lax.all_to_all(outgoing, 'sub', split_axis=0, concat_axis=0, tiled=True)  22.8 us
    ppermute x2, starting transfers between devices, with_halo(): after = lax.ppermute(leading, axis, down)  20.2 us
    ppermute x1, waiting for transfers between devices, passed_along(): return lax.ppermute(value, axis, pairs)  15.3 us
    ppermute x2, waiting for transfers between devices, with_halo(): before = lax.ppermute(last, axis, up)  4.41 us
    ppermute x2, waiting for transfers between devices, with_halo(): after = lax.ppermute(leading, axis, down)  3.66 us
    ppermute x2, starting transfers between devices, with_halo(): before = lax.ppermute(last, axis, up)  3.21 us
    unnamed x8, local copies, waits for them, and re-layouts  2.55 us
    dot_general x1, matrix products, shards(): jnp.einsum('te,ekl->tkl', selector, product, precision=lax.Precision.HIGH...  1.93 us
  transfers between devices with their start and end apart: 5, of which 3 were waited for; matrix products, arithmetic and copies ran while one was open for 2% of the time, Pallas kernels for 0%

commit v1 on v0

v1 whole, which is shorter than its diff:
```python
import jax
import jax.numpy as jnp
from jax import lax
from jax.experimental import pallas as pl
from jax.experimental.pallas import tpu as pltpu
from jax.sharding import PartitionSpec as P

OB_DEV = 8
LANES = 128
GROUP = 8
VMEM = pl.BlockSpec(memory_space=pltpu.VMEM)
SMEM = pl.BlockSpec(memory_space=pltpu.SMEM)


def swap_pairs(count, first):
    pairs = []
    for i in range(first, count - 1, 2):
        pairs += [(i, i + 1), (i + 1, i)]
    return pairs


def xor_pairs(count, mask):
    return [(i, i ^ mask) for i in range(count)]


def product_kernel(
    where_ref, row_ref, code_ref, live_ref, x_ref, pair_ref, beside_ref, next_ref, far_ref, w_ref,
    keep_ref, send_ref, away, xf, source,
):
    sub, band = where_ref[0], where_ref[1]
    fields, rows, width = x_ref.shape
    flat = fields * rows
    capacity = w_ref.shape[0]
    half = keep_ref.shape[0]
    keep_ref[...] = jnp.zeros_like(keep_ref)
    away[...] = jnp.zeros_like(away)

    def full(ref):
        return ref[...].astype(jnp.float32).reshape(flat, width)

    x, pair, beside, near, far = full(x_ref), full(pair_ref), full(beside_ref), full(next_ref), full(far_ref)
    odd_sub, odd_band = sub % 2 == 1, band % 2 == 1
    left, right = jnp.where(odd_sub, pair, beside), jnp.where(odd_sub, beside, pair)
    above, below = jnp.where(odd_band, near, far), jnp.where(odd_band, far, near)
    lane = lax.broadcasted_iota(jnp.int32, (flat, width), 1)
    later = pltpu.roll(jnp.where(lane == 0, right, x), width - 1, 1)
    earlier = pltpu.roll(jnp.where(lane == width - 1, left, x), 1, 1)
    grad_x = 0.5 * (later - earlier)
    xf[0] = x
    xf[1] = grad_x
    xf[2] = above
    xf[3] = below

    def row(which, r):
        return xf[which, pl.ds(r, fields, stride=rows), :]

    for r in range(rows):
        up = row(0, r - 1) if r > 0 else row(2, rows - 1)
        down = row(0, r + 1) if r < rows - 1 else row(3, 0)
        source[r, :, 0:width] = row(0, r).astype(jnp.bfloat16)
        source[r, :, width : 2 * width] = row(1, r).astype(jnp.bfloat16)
        source[r, :, 2 * width : 3 * width] = (0.5 * (down - up)).astype(jnp.bfloat16)

    live = live_ref[0]
    core, along = sub % 2, sub // 2
    for start in range(0, capacity, GROUP):

        @pl.when(start < live)
        def _(start=start):
            for e in range(start, start + GROUP):
                product = jnp.dot(source[row_ref[e]], w_ref[e], preferred_element_type=jnp.float32)
                product = jnp.where(e < live, product, 0.0)
                code = code_ref[e]
                dest = code // 16
                slot = ((dest // 2) ^ along) * 16 + code % 16
                mine = (dest % 2) == core

                @pl.when(mine)
                def _():
                    keep_ref[slot] += product

                @pl.when(jnp.logical_not(mine))
                def _():
                    away[slot] += product

    send_ref[...] = away[...].astype(jnp.bfloat16)


def pair_sum_kernel(keep_ref, got_ref, own_ref, *out_refs):
    count = own_ref.shape[0]
    own_ref[...] = keep_ref[0:count] + got_ref[0:count].astype(jnp.float32)
    for k, out in enumerate(out_refs, 1):
        span = slice(k * count, (k + 1) * count)
        out[...] = (keep_ref[span] + got_ref[span].astype(jnp.float32)).astype(jnp.bfloat16)


def total_kernel(own_ref, *refs):
    got, (here_ref, next_ref) = refs[:-2], refs[-2:]
    total = own_ref[...]
    for ref in got:
        total = total + ref[...].astype(jnp.float32)
    here_ref[...] = total[:OB_DEV]
    next_ref[...] = total[OB_DEV:].astype(jnp.bfloat16)


def final_kernel(here_ref, got_ref, out_ref):
    for q in range(OB_DEV):
        out_ref[:, q * LANES : (q + 1) * LANES] = here_ref[q] + got_ref[q].astype(jnp.float32)


def shards(atmos_flux, weight_tiles, source_row, target_code, live_count):
    fields, rows, width = atmos_flux.shape
    capacity = weight_tiles.shape[2]
    subs, bands = lax.axis_size("sub"), lax.axis_size("band")
    blocks = 2 * OB_DEV
    half = subs // 2 * blocks
    where = jnp.stack([lax.axis_index("sub"), lax.axis_index("band")]).astype(jnp.int32)
    beside = lax.ppermute(atmos_flux, "sub", swap_pairs(subs, 1))
    far = lax.ppermute(atmos_flux, "band", swap_pairs(bands, 1))
    pair = lax.ppermute(atmos_flux, "sub", swap_pairs(subs, 0))
    near = lax.ppermute(atmos_flux, "band", swap_pairs(bands, 0))
    keep, send = pl.pallas_call(
        product_kernel,
        out_shape=(
            jax.ShapeDtypeStruct((half, fields, width), jnp.float32),
            jax.ShapeDtypeStruct((half, fields, width), jnp.bfloat16),
        ),
        in_specs=[SMEM] * 4 + [VMEM] * 6,
        out_specs=(VMEM, VMEM),
        scratch_shapes=[
            pltpu.VMEM((half, fields, width), jnp.float32),
            pltpu.VMEM((4, fields * rows, width), jnp.float32),
            pltpu.VMEM((rows, fields, 3 * width), jnp.bfloat16),
        ],
        compiler_params=pltpu.CompilerParams(vmem_limit_bytes=24 * 2**20),
        name="product",
    )(
        where, source_row[0, 0], target_code[0, 0], live_count[0], atmos_flux, pair, beside, near, far,
        weight_tiles[0, 0],
    )
    got = lax.ppermute(send, "sub", xor_pairs(subs, 1))
    chunk = jax.ShapeDtypeStruct((blocks, fields, width), jnp.bfloat16)
    own, *outs = pl.pallas_call(
        pair_sum_kernel,
        out_shape=(jax.ShapeDtypeStruct(chunk.shape, jnp.float32),) + (chunk,) * (subs // 2 - 1),
        in_specs=[VMEM] * 2,
        out_specs=(VMEM,) * (subs // 2),
        compiler_params=pltpu.CompilerParams(vmem_limit_bytes=24 * 2**20),
        name="pair_sum",
    )(keep, got)
    arrived = [lax.ppermute(outs[k - 1], "sub", xor_pairs(subs, 2 * k)) for k in (2, 1, 3)]
    here, ahead = pl.pallas_call(
        total_kernel,
        out_shape=(
            jax.ShapeDtypeStruct((OB_DEV, fields, width), jnp.float32),
            jax.ShapeDtypeStruct((OB_DEV, fields, width), jnp.bfloat16),
        ),
        in_specs=[VMEM] * (subs // 2),
        out_specs=(VMEM, VMEM),
        compiler_params=pltpu.CompilerParams(vmem_limit_bytes=24 * 2**20),
        name="total",
    )(own, *arrived)
    behind = lax.ppermute(ahead, "band", [(i, (i + 1) % bands) for i in range(bands)])
    return pl.pallas_call(
        final_kernel,
        out_shape=jax.ShapeDtypeStruct((fields, OB_DEV * width), jnp.float32),
        in_specs=[VMEM] * 2,
        out_specs=VMEM,
        compiler_params=pltpu.CompilerParams(vmem_limit_bytes=24 * 2**20),
        name="final",
    )(here, behind)


def solution(mesh):
    return jax.shard_map(
        shards,
        mesh=mesh,
        in_specs=(
            P(None, "band", "sub"),
            P("band", "sub", None, None, None),
            P("band", "sub", None),
            P("band", "sub", None),
            P("band", "sub"),
        ),
        out_specs=P(None, ("band", "sub")),
        check_vma=False,
    )
```

time: 82 us -> 67.8 us (0.83)
  blocking collectives: 22.8 us -> 0 us
  starting transfers between devices: 25.4 us -> 42.7 us
  waiting for transfers between devices: 23.4 us -> 15.8 us
  Pallas kernels: 0 us -> 3.98 us
  matrix products: 3.71 us -> 0 us
  other arithmetic: 1.16 us -> 0.08 us
    all_to_all x1 -> x0, blocking collectives: 22.8 us -> none  [shards(): lax.all_to_all(outgoing, 'sub', split_axis=0, concat_axis=0, tiled=True)]
    ppermute x5 -> x9, starting transfers between devices: 25.4 us -> 42.7 us  [the longest x1 18 us: shards(): far = lax.ppermute(atmos_flux, 'band', swap_pairs(bands, 1))]
    ppermute x5 -> x9, waiting for transfers between devices: 23.4 us -> 15.8 us  [the longest x1 6.34 us: shards(): lax.ppermute(ahead, 'band', [(i, (i + 1) % bands) for i in range(bands)])]
    pallas_call x0 -> x4, Pallas kernels: none -> 3.98 us  [the longest x1 3.12 us: shards(): pl.pallas_call(product_kernel, out_shape=(jax.ShapeDtypeStruct((half, fie...]
    dot_general x2 -> x0, matrix products: 3.71 us -> none  [the longest x1 1.93 us: shards(): jnp.einsum('te,ekl->tkl', selector, product, precision=lax.Precision.HIGH...]
    gather x1 -> x0, local copies, waits for them, and re-layouts: 1.54 us -> none  [shards(): picked = operand[source_row[0, 0]]]
    unnamed x8, local copies, waits for them, and re-layouts: 2.55 us -> 4.04 us
  transfers between devices with their start and end apart: 5 -> 9, of which waited for: 3 -> 5; matrix products, arithmetic and copies ran while one was open for 2% -> 0% of each run, Pallas kernels for 0% -> 0%
where the time goes in v1:
time: 67.8 us; the launch traced here: 67.3 us
  starting transfers between devices  42.7 us (63%)
  waiting for transfers between devices  15.8 us (23%)
  local copies, waits for them, and re-layouts  4.04 us (6%)
  Pallas kernels  3.98 us (6%)
  between operations  0.76 us (1%)
    ppermute x1, starting transfers between devices, shards(): far = lax.ppermute(atmos_flux, 'band', swap_pairs(bands, 1))  18 us
    ppermute x3, starting transfers between devices, shards(): lax.ppermute(outs[k - 1], 'sub', xor_pairs(subs, 2 * k))  11.5 us
    ppermute x1, waiting for transfers between devices, shards(): lax.ppermute(ahead, 'band', [(i, (i + 1) % bands) for i in range(bands)])  6.34 us
    ppermute x3, waiting for transfers between devices, shards(): lax.ppermute(outs[k - 1], 'sub', xor_pairs(subs, 2 * k))  5.87 us
    ppermute x1, starting transfers between devices, shards(): pair = lax.ppermute(atmos_flux, 'sub', swap_pairs(subs, 0))  4.85 us
    unnamed x8, local copies, waits for them, and re-layouts  4.04 us
    ppermute x1, starting transfers between devices, shards(): near = lax.ppermute(atmos_flux, 'band', swap_pairs(bands, 0))  3.82 us
    pallas_call x1, Pallas kernels, shards(): pl.pallas_call(product_kernel, out_shape=(jax.ShapeDtypeStruct((half, fie...  3.12 us
  transfers between devices with their start and end apart: 9, of which 5 were waited for; matrix products, arithmetic and copies ran while one was open for 0% of the time, Pallas kernels for 0%

profile of v1, /device:TPU:6, one launch (start us, length us, event | category | flops | bytes accessed | tf_op | source)
XLA Modules:
  0.0 67.3 jit_solution(2302867644660900043)
XLA Ops:
  0.0 3.8 %collective-permute-start.2 = (bf16[32,8,128]{2,1,0:T(8,128)(2,1)}, bf16[32,8,128]{2,1,0:T(8,128)(2,1)S(1)}, u32[]{:S(2)}, u32[]{:S(2)}) collective-permute-start(bf16[32,8,128]{2,1,0:T(8,128)(2,1)} %x_ref.1), channel_id=1, source_target_pairs={{0,8},{8,0},{16,24},{24,16},{32,40},{40,32},{48,56},{56,48},{64,72... | collective-permute-start | bytes 196616 | tf_op jit(solution)/shard_map/ppermute | solution.py:121
  3.8 0.7 collective-permute-start.1
  4.5 4.8 %collective-permute-start = (bf16[32,8,128]{2,1,0:T(8,128)(2,1)}, bf16[32,8,128]{2,1,0:T(8,128)(2,1)S(1)}, u32[]{:S(2)}, u32[]{:S(2)}) collective-permute-start(bf16[32,8,128]{2,1,0:T(8,128)(2,1)} %x_ref.1), channel_id=1, source_target_pairs={{0,1},{1,0},{2,3},{3,2},{4,5},{5,4},{6,7},{7,6},{8,9},{9,8},{10,11... | collective-permute-start | bytes 196616 | tf_op jit(solution)/shard_map/ppermute | solution.py:120
  9.4 18.0 %collective-permute-start.3 = (bf16[32,8,128]{2,1,0:T(8,128)(2,1)}, bf16[32,8,128]{2,1,0:T(8,128)(2,1)S(1)}, u32[]{:S(2)}, u32[]{:S(2)}) collective-permute-start(bf16[32,8,128]{2,1,0:T(8,128)(2,1)} %x_ref.1), channel_id=1, source_target_pairs={{8,16},{16,8},{24,32},{32,24},{40,48},{48,40},{56,64},{64,56},{72,... | collective-permute-start | bytes 196616 | tf_op jit(solution)/shard_map/ppermute | solution.py:119
  28.0 0.1 pad_add_fusion.where_ref
  28.1 0.0 collective-permute-done.2.next_ref
  28.1 0.0 collective-permute-done.1.beside_ref
  28.1 0.0 collective-permute-done.pair_ref
  28.1 1.7 %collective-permute-done.3.far_ref = bf16[32,8,128]{2,1,0:T(8,128)(2,1)S(1)} collective-permute-done((bf16[32,8,128]{2,1,0:T(8,128)(2,1)}, bf16[32,8,128]{2,1,0:T(8,128)(2,1)S(1)}, u32[]{:S(2)}, u32[]{:S(2)}) %collective-permute-start.3) | collective-permute-done | bytes 65568 | tf_op jit(solution)/shard_map/ppermute | solution.py:119
  29.9 0.0 copy-start
  29.9 1.9 %copy-done = bf16[1,1,32,384,128]{4,3,2,1,0:T(8,128)(2,1)S(1)} copy-done((bf16[1,1,32,384,128]{4,3,2,1,0:T(8,128)(2,1)S(1)}, bf16[1,1,32,384,128]{4,3,2,1,0:T(8,128)(2,1)}, u32[]{:S(2)}) %copy-start) | copy-done | bytes 3145752
  31.8 0.0 copy-start.1
  31.8 0.8 %copy-done.1 = bf16[32,8,128]{2,1,0:T(8,128)(2,1)S(1)} copy-done((bf16[32,8,128]{2,1,0:T(8,128)(2,1)S(1)}, bf16[32,8,128]{2,1,0:T(8,128)(2,1)}, u32[]{:S(2)}) %copy-start.1) | copy-done | bytes 65560
  32.6 0.0 copy-start.2
  32.6 0.7 copy-done.2
  33.2 0.0 copy-start.3
  33.2 0.7 copy-done.3
  33.9 3.1 %product.1 = (f32[64,32,128]{2,1,0:T(8,128)S(1)}, bf16[64,32,128]{2,1,0:T(8,128)(2,1)S(1)}) custom-call(s32[2]{0:T(128)S(1)} %pad_add_fusion.where_ref, s32[32]{0:T(128)S(1)} %bitcast.8, s32[32]{0:T(128)S(1)} %bitcast.9, s32[1]{0:T(128)} %bitcast.6.live_ref, bf16[32,8,128]{2,1,0:T(8,128)(2,1)S(1)} %copy-done.1, ...), custom_call_target="tpu_custom_call" | custom-call | tf_op jit(solution)/shard_map/product/pallas_call | solution.py:122
  37.0 1.9 %collective-permute-start.4 = (bf16[64,32,128]{2,1,0:T(8,128)(2,1)S(1)}, bf16[64,32,128]{2,1,0:T(8,128)(2,1)S(1)}, u32[]{:S(2)}, u32[]{:S(2)}) collective-permute-start(bf16[64,32,128]{2,1,0:T(8,128)(2,1)S(1)} %get-tuple-element.14), channel_id=1, source_target_pairs={{0,1},{1,0},{2,3},{3,2},{4,5},{5,4},{6,7},{7,6},{8,9},{9,8},{10,11... | collective-permute-start | bytes 1572872 | tf_op jit(solution)/shard_map/ppermute | solution.py:141
  39.0 1.9 %collective-permute-done.4.got_ref = bf16[64,32,128]{2,1,0:T(8,128)(2,1)S(1)} collective-permute-done((bf16[64,32,128]{2,1,0:T(8,128)(2,1)S(1)}, bf16[64,32,128]{2,1,0:T(8,128)(2,1)S(1)}, u32[]{:S(2)}, u32[]{:S(2)}) %collective-permute-start.4) | collective-permute-done | bytes 524320 | tf_op jit(solution)/shard_map/ppermute | solution.py:141
  40.8 0.1 pair_sum.1
  41.0 7.1 %collective-permute-start.5 = (bf16[16,32,128]{2,1,0:T(8,128)(2,1)S(1)}, bf16[16,32,128]{2,1,0:T(8,128)(2,1)S(1)}, u32[]{:S(2)}, u32[]{:S(2)}) collective-permute-start(bf16[16,32,128]{2,1,0:T(8,128)(2,1)S(1)} %get-tuple-element.16), channel_id=1, source_target_pairs={{0,4},{1,5},{2,6},{3,7},{4,0},{5,1},{6,2},{7,3},{8,12},{9,13},{10,... | collective-permute-start | bytes 393224 | tf_op jit(solution)/shard_map/ppermute | solution.py:151
  48.0 1.9 %collective-permute-start.6 = (bf16[16,32,128]{2,1,0:T(8,128)(2,1)S(1)}, bf16[16,32,128]{2,1,0:T(8,128)(2,1)S(1)}, u32[]{:S(2)}, u32[]{:S(2)}) collective-permute-start(bf16[16,32,128]{2,1,0:T(8,128)(2,1)S(1)} %get-tuple-element.17), channel_id=1, source_target_pairs={{0,2},{1,3},{2,0},{3,1},{4,6},{5,7},{6,4},{7,5},{8,10},{9,11},{10,... | collective-permute-start | bytes 393224 | tf_op jit(solution)/shard_map/ppermute | solution.py:151
  50.0 2.5 %collective-permute-start.7 = (bf16[16,32,128]{2,1,0:T(8,128)(2,1)S(1)}, bf16[16,32,128]{2,1,0:T(8,128)(2,1)S(1)}, u32[]{:S(2)}, u32[]{:S(2)}) collective-permute-start(bf16[16,32,128]{2,1,0:T(8,128)(2,1)S(1)} %get-tuple-element.18), channel_id=1, source_target_pairs={{0,6},{1,7},{2,4},{3,5},{4,2},{5,3},{6,0},{7,1},{8,14},{9,15},{10,... | collective-permute-start | bytes 393224 | tf_op jit(solution)/shard_map/ppermute | solution.py:151
  52.5 0.0 collective-permute-done.5.refs_0_
  52.5 2.7 %collective-permute-done.6.refs_1_ = bf16[16,32,128]{2,1,0:T(8,128)(2,1)S(1)} collective-permute-done((bf16[16,32,128]{2,1,0:T(8,128)(2,1)S(1)}, bf16[16,32,128]{2,1,0:T(8,128)(2,1)S(1)}, u32[]{:S(2)}, u32[]{:S(2)}) %collective-permute-start.6) | collective-permute-done | bytes 131104 | tf_op jit(solution)/shard_map/ppermute | solution.py:151
  55.2 3.1 %collective-permute-done.7.refs_2_ = bf16[16,32,128]{2,1,0:T(8,128)(2,1)S(1)} collective-permute-done((bf16[16,32,128]{2,1,0:T(8,128)(2,1)S(1)}, bf16[16,32,128]{2,1,0:T(8,128)(2,1)S(1)}, u32[]{:S(2)}, u32[]{:S(2)}) %collective-permute-start.7) | collective-permute-done | bytes 131104 | tf_op jit(solution)/shard_map/ppermute | solution.py:151
  58.3 0.1 total.1
  58.4 1.9 %collective-permute-start.8 = (bf16[8,32,128]{2,1,0:T(8,128)(2,1)S(1)}, bf16[8,32,128]{2,1,0:T(8,128)(2,1)S(1)}, u32[]{:S(2)}, u32[]{:S(2)}) collective-permute-start(bf16[8,32,128]{2,1,0:T(8,128)(2,1)S(1)} %get-tuple-element.20), channel_id=1, source_target_pairs={{0,8},{8,16},{16,24},{24,32},{32,40},{40,48},{48,56},{56,64},{64,7... | collective-permute-start | bytes 196616 | tf_op jit(solution)/shard_map/ppermute | solution.py:163
  60.3 6.3 %collective-permute-done.8.got_ref = bf16[8,32,128]{2,1,0:T(8,128)(2,1)S(1)} collective-permute-done((bf16[8,32,128]{2,1,0:T(8,128)(2,1)S(1)}, bf16[8,32,128]{2,1,0:T(8,128)(2,1)S(1)}, u32[]{:S(2)}, u32[]{:S(2)}) %collective-permute-start.8) | collective-permute-done | bytes 65568 | tf_op jit(solution)/shard_map/ppermute | solution.py:163
  66.7 0.7 final.1
Async XLA Ops:
  0.0 28.1 %collective-permute-start.2 = (bf16[32,8,128]{2,1,0:T(8,128)(2,1)}, bf16[32,8,128]{2,1,0:T(8,128)(2,1)S(1)}, u32[]{:S(2)}, u32[]{:S(2)}) collective-permute-start(bf16[32,8,128]{2,1,0:T(8,128)(2,1)} %x_ref.1), channel_id=1, source_target_pairs={{0,8},{8,0},{16,24},{24,16},{32,40},{40,32},{48,56},{56,48},{64,72... | collective-permute-start | bytes 196616 | tf_op jit(solution)/shard_map/ppermute | solution.py:121
  3.8 24.3 %collective-permute-start.1 = (bf16[32,8,128]{2,1,0:T(8,128)(2,1)}, bf16[32,8,128]{2,1,0:T(8,128)(2,1)S(1)}, u32[]{:S(2)}, u32[]{:S(2)}) collective-permute-start(bf16[32,8,128]{2,1,0:T(8,128)(2,1)} %x_ref.1), channel_id=1, source_target_pairs={{1,2},{2,1},{3,4},{4,3},{5,6},{6,5},{9,10},{10,9},{11,12},{12,11},... | collective-permute-start | bytes 196616 | tf_op jit(solution)/shard_map/ppermute | solution.py:118
  4.5 23.6 %collective-permute-start = (bf16[32,8,128]{2,1,0:T(8,128)(2,1)}, bf16[32,8,128]{2,1,0:T(8,128)(2,1)S(1)}, u32[]{:S(2)}, u32[]{:S(2)}) collective-permute-start(bf16[32,8,128]{2,1,0:T(8,128)(2,1)} %x_ref.1), channel_id=1, source_target_pairs={{0,1},{1,0},{2,3},{3,2},{4,5},{5,4},{6,7},{7,6},{8,9},{9,8},{10,11... | collective-permute-start | bytes 196616 | tf_op jit(solution)/shard_map/ppermute | solution.py:120
  9.4 20.5 %collective-permute-start.3 = (bf16[32,8,128]{2,1,0:T(8,128)(2,1)}, bf16[32,8,128]{2,1,0:T(8,128)(2,1)S(1)}, u32[]{:S(2)}, u32[]{:S(2)}) collective-permute-start(bf16[32,8,128]{2,1,0:T(8,128)(2,1)} %x_ref.1), channel_id=1, source_target_pairs={{8,16},{16,8},{24,32},{32,24},{40,48},{48,40},{56,64},{64,56},{72,... | collective-permute-start | bytes 196616 | tf_op jit(solution)/shard_map/ppermute | solution.py:119
  29.9 1.9 %copy-start = (bf16[1,1,32,384,128]{4,3,2,1,0:T(8,128)(2,1)S(1)}, bf16[1,1,32,384,128]{4,3,2,1,0:T(8,128)(2,1)}, u32[]{:S(2)}) copy-start(bf16[1,1,32,384,128]{4,3,2,1,0:T(8,128)(2,1)} %param.6) | copy-start | bytes 9437188
  31.8 0.8 %copy-start.1 = (bf16[32,8,128]{2,1,0:T(8,128)(2,1)S(1)}, bf16[32,8,128]{2,1,0:T(8,128)(2,1)}, u32[]{:S(2)}) copy-start(bf16[32,8,128]{2,1,0:T(8,128)(2,1)} %x_ref.1) | copy-start | bytes 196612
  32.6 0.7 copy-start.2
  33.2 0.7 copy-start.3
  37.0 3.8 %collective-permute-start.4 = (bf16[64,32,128]{2,1,0:T(8,128)(2,1)S(1)}, bf16[64,32,128]{2,1,0:T(8,128)(2,1)S(1)}, u32[]{:S(2)}, u32[]{:S(2)}) collective-permute-start(bf16[64,32,128]{2,1,0:T(8,128)(2,1)S(1)} %get-tuple-element.14), channel_id=1, source_target_pairs={{0,1},{1,0},{2,3},{3,2},{4,5},{5,4},{6,7},{7,6},{8,9},{9,8},{10,11... | collective-permute-start | bytes 1572872 | tf_op jit(solution)/shard_map/ppermute | solution.py:141
  41.0 11.5 %collective-permute-start.5 = (bf16[16,32,128]{2,1,0:T(8,128)(2,1)S(1)}, bf16[16,32,128]{2,1,0:T(8,128)(2,1)S(1)}, u32[]{:S(2)}, u32[]{:S(2)}) collective-permute-start(bf16[16,32,128]{2,1,0:T(8,128)(2,1)S(1)} %get-tuple-element.16), channel_id=1, source_target_pairs={{0,4},{1,5},{2,6},{3,7},{4,0},{5,1},{6,2},{7,3},{8,12},{9,13},{10,... | collective-permute-start | bytes 393224 | tf_op jit(solution)/shard_map/ppermute | solution.py:151
  48.0 7.2 %collective-permute-start.6 = (bf16[16,32,128]{2,1,0:T(8,128)(2,1)S(1)}, bf16[16,32,128]{2,1,0:T(8,128)(2,1)S(1)}, u32[]{:S(2)}, u32[]{:S(2)}) collective-permute-start(bf16[16,32,128]{2,1,0:T(8,128)(2,1)S(1)} %get-tuple-element.17), channel_id=1, source_target_pairs={{0,2},{1,3},{2,0},{3,1},{4,6},{5,7},{6,4},{7,5},{8,10},{9,11},{10,... | collective-permute-start | bytes 393224 | tf_op jit(solution)/shard_map/ppermute | solution.py:151
  50.0 8.4 %collective-permute-start.7 = (bf16[16,32,128]{2,1,0:T(8,128)(2,1)S(1)}, bf16[16,32,128]{2,1,0:T(8,128)(2,1)S(1)}, u32[]{:S(2)}, u32[]{:S(2)}) collective-permute-start(bf16[16,32,128]{2,1,0:T(8,128)(2,1)S(1)} %get-tuple-element.18), channel_id=1, source_target_pairs={{0,6},{1,7},{2,4},{3,5},{4,2},{5,3},{6,0},{7,1},{8,14},{9,15},{10,... | collective-permute-start | bytes 393224 | tf_op jit(solution)/shard_map/ppermute | solution.py:151
  58.4 8.3 %collective-permute-start.8 = (bf16[8,32,128]{2,1,0:T(8,128)(2,1)S(1)}, bf16[8,32,128]{2,1,0:T(8,128)(2,1)S(1)}, u32[]{:S(2)}, u32[]{:S(2)}) collective-permute-start(bf16[8,32,128]{2,1,0:T(8,128)(2,1)S(1)} %get-tuple-element.20), channel_id=1, source_target_pairs={{0,8},{8,16},{16,24},{24,32},{32,40},{40,48},{48,56},{56,64},{64,7... | collective-permute-start | bytes 196616 | tf_op jit(solution)/shard_map/ppermute | solution.py:163

commit v2 on v1

v2 whole, which is shorter than its diff:
```python
import jax
import jax.numpy as jnp
from jax import lax
from jax.experimental import pallas as pl
from jax.experimental.pallas import tpu as pltpu
from jax.sharding import PartitionSpec as P

OB_DEV = 8
LANES = 128
GROUP = 8
VMEM = pl.BlockSpec(memory_space=pltpu.VMEM)
SMEM = pl.BlockSpec(memory_space=pltpu.SMEM)


def swap_pairs(count, first):
    pairs = []
    for i in range(first, count - 1, 2):
        pairs += [(i, i + 1), (i + 1, i)]
    return pairs


def xor_pairs(count, mask):
    return [(i, i ^ mask) for i in range(count)]


def edge_kernel(x_ref, pair_ref, cross_ref):
    odd = lax.axis_index("band") % 2 == 1
    fields, rows, width = x_ref.shape
    x = x_ref[...].astype(jnp.float32)
    first, last = x[:, 0, :], x[:, rows - 1, :]
    pair_ref[...] = jnp.where(odd, first, last).astype(jnp.bfloat16)
    cross_ref[...] = jnp.where(odd, last, first).astype(jnp.bfloat16)


def entry(info_ref, e, live):
    core, along = lax.axis_index("sub") % 2, lax.axis_index("sub") // 2
    packed = info_ref[e]
    code = packed // 8
    dest = code // 16
    slot = ((dest % 2) ^ core) * 64 + ((dest // 2) ^ along) * 16 + code % 16
    return packed % 8, jnp.where(e < live, slot, 128)


def inner_kernel(info_ref, x_ref, w_hbm, acc_ref, w_ref, xf, source, sems):
    fields, rows, width = x_ref.shape
    flat = fields * rows
    capacity = w_ref.shape[0]
    live = info_ref[capacity]

    def load(start):
        span = pl.ds(start, GROUP)
        return pltpu.make_async_copy(w_hbm.at[span], w_ref.at[span], sems.at[start // GROUP])

    for start in range(0, capacity, GROUP):
        pl.when(start < live)(lambda start=start: load(start).start())
    acc_ref[...] = jnp.zeros_like(acc_ref)
    x = x_ref[...].astype(jnp.float32).reshape(flat, width)
    lane = lax.broadcasted_iota(jnp.int32, (flat, width), 1)
    later = pltpu.roll(jnp.where(lane == 0, 0.0, x), width - 1, 1)
    earlier = pltpu.roll(jnp.where(lane == width - 1, 0.0, x), 1, 1)
    xf[0] = x
    xf[1] = 0.5 * (later - earlier)

    def row(which, r):
        return xf[which, pl.ds(r, fields, stride=rows), :]

    for r in range(rows):
        up = row(0, r - 1) if r > 0 else 0.0
        down = row(0, r + 1) if r < rows - 1 else 0.0
        source[r, :, 0:width] = row(0, r).astype(jnp.bfloat16)
        source[r, :, width : 2 * width] = row(1, r).astype(jnp.bfloat16)
        source[r, :, 2 * width : 3 * width] = (0.5 * (down - up)).astype(jnp.bfloat16)

    for start in range(0, capacity, GROUP):

        @pl.when(start < live)
        def _(start=start):
            load(start).wait()
            for e in range(start, start + GROUP):
                r, slot = entry(info_ref, e, live)
                acc_ref[slot] += jnp.dot(source[r], w_ref[e], preferred_element_type=jnp.float32)


def border_kernel(info_ref, pair_ref, beside_ref, near_ref, far_ref, w_ref, acc_in, acc_ref, send_ref, xf, side, ends):
    del acc_in
    fields, rows, width = pair_ref.shape
    flat = fields * rows
    capacity = w_ref.shape[0]
    live = info_ref[capacity]
    odd_sub, odd_band = lax.axis_index("sub") % 2 == 1, lax.axis_index("band") % 2 == 1
    pair, beside = (ref[...].astype(jnp.float32).reshape(flat, width) for ref in (pair_ref, beside_ref))
    left = jnp.where(odd_sub, pair, beside)[:, width - 1 : width]
    right = jnp.where(odd_sub, beside, pair)[:, 0:1]
    xf[0] = jnp.broadcast_to(-0.5 * left, (flat, width))
    xf[1] = jnp.broadcast_to(0.5 * right, (flat, width))
    for r in range(rows):
        for which in range(2):
            side[which, r] = xf[which, pl.ds(r, fields, stride=rows), :]
    near, far = near_ref[...].astype(jnp.float32), far_ref[...].astype(jnp.float32)
    ends[...] = jnp.zeros_like(ends)
    ends[0] = (-0.5 * jnp.where(odd_band, near, far)).astype(jnp.bfloat16)
    ends[rows - 1] = (0.5 * jnp.where(odd_band, far, near)).astype(jnp.bfloat16)
    for start in range(0, capacity, GROUP):

        @pl.when(start < live)
        def _(start=start):
            for e in range(start, start + GROUP):
                r, slot = entry(info_ref, e, live)
                first = w_ref[e, width : width + 16, :].astype(jnp.float32)[0:1]
                last = w_ref[e, 2 * width - 16 : 2 * width, :].astype(jnp.float32)[15:16]
                acc_ref[slot] += (
                    jnp.dot(ends[r], w_ref[e, 2 * width : 3 * width, :], preferred_element_type=jnp.float32)
                    + side[0, r] * first
                    + side[1, r] * last
                )

    half = send_ref.shape[0]
    send_ref[...] = acc_ref[half : 2 * half].astype(jnp.bfloat16)


def pair_sum_kernel(keep_ref, got_ref, own_ref, *out_refs):
    count = own_ref.shape[0]
    own_ref[...] = keep_ref[0:count] + got_ref[0:count].astype(jnp.float32)
    for k, out in enumerate(out_refs, 1):
        span = slice(k * count, (k + 1) * count)
        out[...] = (keep_ref[span] + got_ref[span].astype(jnp.float32)).astype(jnp.bfloat16)


def total_kernel(own_ref, *refs):
    got, (here_ref, next_ref) = refs[:-2], refs[-2:]
    total = own_ref[...]
    for ref in got:
        total = total + ref[...].astype(jnp.float32)
    here_ref[...] = total[:OB_DEV]
    next_ref[...] = total[OB_DEV:].astype(jnp.bfloat16)


def final_kernel(here_ref, got_ref, out_ref):
    for q in range(OB_DEV):
        out_ref[:, q * LANES : (q + 1) * LANES] = here_ref[q] + got_ref[q].astype(jnp.float32)


def shards(atmos_flux, weight_tiles, source_row, target_code, live_count):
    fields, rows, width = atmos_flux.shape
    capacity = weight_tiles.shape[2]
    subs, bands = lax.axis_size("sub"), lax.axis_size("band")
    blocks = 2 * OB_DEV
    half = subs // 2 * blocks
    params = pltpu.CompilerParams(vmem_limit_bytes=24 * 2**20)
    info = jnp.concatenate([source_row[0, 0] + 8 * target_code[0, 0], live_count[0]])
    pair = lax.ppermute(atmos_flux, "sub", swap_pairs(subs, 0))
    beside = lax.ppermute(atmos_flux, "sub", swap_pairs(subs, 1))
    edge = jax.ShapeDtypeStruct((fields, width), jnp.bfloat16)
    pair_edge, cross_edge = pl.pallas_call(
        edge_kernel,
        out_shape=(edge, edge),
        in_specs=[VMEM],
        out_specs=(VMEM, VMEM),
        compiler_params=params,
        name="edges",
    )(atmos_flux)
    near = lax.ppermute(pair_edge, "band", swap_pairs(bands, 0))
    far = lax.ppermute(cross_edge, "band", swap_pairs(bands, 1))
    sums = jax.ShapeDtypeStruct((2 * half + 1, fields, width), jnp.float32)
    tiles = pltpu.with_memory_space_constraint(weight_tiles[0, 0], pltpu.HBM)
    acc, held = pl.pallas_call(
        inner_kernel,
        out_shape=(sums, jax.ShapeDtypeStruct(tiles.shape, tiles.dtype)),
        in_specs=[SMEM, VMEM, pl.BlockSpec(memory_space=pltpu.HBM)],
        out_specs=(VMEM, VMEM),
        scratch_shapes=[
            pltpu.VMEM((2, fields * rows, width), jnp.float32),
            pltpu.VMEM((rows, fields, 3 * width), jnp.bfloat16),
            pltpu.SemaphoreType.DMA((capacity // GROUP,)),
        ],
        compiler_params=params,
        cost_estimate=pl.CostEstimate(flops=100_000_000, bytes_accessed=6_000_000, transcendentals=0),
        name="inner",
    )(info, atmos_flux, tiles)
    acc, send = pl.pallas_call(
        border_kernel,
        out_shape=(sums, jax.ShapeDtypeStruct((half, fields, width), jnp.bfloat16)),
        in_specs=[SMEM] + [VMEM] * 6,
        out_specs=(VMEM, VMEM),
        scratch_shapes=[
            pltpu.VMEM((2, fields * rows, width), jnp.float32),
            pltpu.VMEM((2, rows, fields, width), jnp.float32),
            pltpu.VMEM((rows, fields, width), jnp.bfloat16),
        ],
        input_output_aliases={6: 0},
        compiler_params=params,
        name="border",
    )(info, pair, beside, near, far, held, acc)
    got = lax.ppermute(send, "sub", xor_pairs(subs, 1))
    chunk = jax.ShapeDtypeStruct((blocks, fields, width), jnp.bfloat16)
    own, *outs = pl.pallas_call(
        pair_sum_kernel,
        out_shape=(jax.ShapeDtypeStruct(chunk.shape, jnp.float32),) + (chunk,) * (subs // 2 - 1),
        in_specs=[VMEM] * 2,
        out_specs=(VMEM,) * (subs // 2),
        compiler_params=params,
        name="pair_sum",
    )(acc, got)
    arrived = [lax.ppermute(outs[k - 1], "sub", xor_pairs(subs, 2 * k)) for k in (2, 1, 3)]
    here, ahead = pl.pallas_call(
        total_kernel,
        out_shape=(
            jax.ShapeDtypeStruct((OB_DEV, fields, width), jnp.float32),
            jax.ShapeDtypeStruct((OB_DEV, fields, width), jnp.bfloat16),
        ),
        in_specs=[VMEM] * (subs // 2),
        out_specs=(VMEM, VMEM),
        compiler_params=params,
        name="total",
    )(own, *arrived)
    behind = lax.ppermute(ahead, "band", [(i, (i + 1) % bands) for i in range(bands)])
    return pl.pallas_call(
        final_kernel,
        out_shape=jax.ShapeDtypeStruct((fields, OB_DEV * width), jnp.float32),
        in_specs=[VMEM] * 2,
        out_specs=VMEM,
        compiler_params=params,
        name="final",
    )(here, behind)


def solution(mesh):
    return jax.shard_map(
        shards,
        mesh=mesh,
        in_specs=(
            P(None, "band", "sub"),
            P("band", "sub", None, None, None),
            P("band", "sub", None),
            P("band", "sub", None),
            P("band", "sub"),
        ),
        out_specs=P(None, ("band", "sub")),
        check_vma=False,
    )
```

time: 67.8 us -> 61.6 us (0.909)
  local copies, waits for them, and re-layouts: 4.04 us -> 0.83 us
  waiting for transfers between devices: 15.8 us -> 13.3 us
  starting transfers between devices: 42.7 us -> 41.6 us
    unnamed x8 -> x2, local copies, waits for them, and re-layouts: 4.04 us -> 0.83 us
    ppermute x2, waiting for transfers between devices: 1.73 us -> 0.01 us  [the longest x1 0.01 us: shards(): near = lax.ppermute(pair_edge, 'band', swap_pairs(bands, 0))]
    ppermute x3, starting transfers between devices: 11.5 us -> 10.4 us  [shards(): lax.ppermute(outs[k - 1], 'sub', xor_pairs(subs, 2 * k))]
    ppermute x3, waiting for transfers between devices: 5.87 us -> 5.09 us  [shards(): lax.ppermute(outs[k - 1], 'sub', xor_pairs(subs, 2 * k))]
    pallas_call x1 -> x3, Pallas kernels: 3.12 us -> 3.02 us  [the longest x1 1.97 us: shards(): pl.pallas_call(inner_kernel, out_shape=(sums, jax.ShapeDtypeStruct(tiles....]
  transfers between devices with their start and end apart: 9 -> 9, of which waited for: 5 -> 4; matrix products, arithmetic and copies ran while one was open for 0% -> 1% of each run, Pallas kernels for 0% -> 3%
where the time goes in v2:
time: 61.6 us; the launch traced here: 61.2 us
  starting transfers between devices  41.6 us (68%)
  waiting for transfers between devices  13.3 us (22%)
  Pallas kernels  3.86 us (6%)
  local copies, waits for them, and re-layouts  0.83 us (1%)
  between operations  0.8 us (1%)
  other arithmetic  0.75 us (1%)
    ppermute x1, starting transfers between devices, shards(): far = lax.ppermute(cross_edge, 'band', swap_pairs(bands, 1))  18 us
    ppermute x3, starting transfers between devices, shards(): lax.ppermute(outs[k - 1], 'sub', xor_pairs(subs, 2 * k))  10.4 us
    ppermute x1, waiting for transfers between devices, shards(): lax.ppermute(ahead, 'band', [(i, (i + 1) % bands) for i in range(bands)])  6.34 us
    ppermute x3, waiting for transfers between devices, shards(): lax.ppermute(outs[k - 1], 'sub', xor_pairs(subs, 2 * k))  5.09 us
    ppermute x1, starting transfers between devices, shards(): pair = lax.ppermute(atmos_flux, 'sub', swap_pairs(subs, 0))  4.84 us
    ppermute x1, starting transfers between devices, shards(): near = lax.ppermute(pair_edge, 'band', swap_pairs(bands, 0))  3.83 us
    pallas_call x1, Pallas kernels, shards(): pl.pallas_call(inner_kernel, out_shape=(sums, jax.ShapeDtypeStruct(tiles....  1.97 us
    ppermute x1, starting transfers between devices, shards(): got = lax.ppermute(send, 'sub', xor_pairs(subs, 1))  1.92 us
  transfers between devices with their start and end apart: 9, of which 4 were waited for; matrix products, arithmetic and copies ran while one was open for 1% of the time, Pallas kernels for 3%

profile of v2, /device:TPU:6, one launch (start us, length us, event | category | flops | bytes accessed | tf_op | source)
XLA Modules:
  0.0 61.2 jit_solution(1587284133938325542)
XLA Ops:
  0.0 0.7 %collective-permute-start.1 = (bf16[32,8,128]{2,1,0:T(8,128)(2,1)}, bf16[32,8,128]{2,1,0:T(8,128)(2,1)S(1)}, u32[]{:S(2)}, u32[]{:S(2)}) collective-permute-start(bf16[32,8,128]{2,1,0:T(8,128)(2,1)} %x_ref.3), channel_id=1, source_target_pairs={{1,2},{2,1},{3,4},{4,3},{5,6},{6,5},{9,10},{10,9},{11,12},{12,11},... | collective-permute-start | bytes 196616 | tf_op jit(solution)/shard_map/ppermute | solution.py:152
  0.7 4.8 %collective-permute-start = (bf16[32,8,128]{2,1,0:T(8,128)(2,1)}, bf16[32,8,128]{2,1,0:T(8,128)(2,1)S(1)}, u32[]{:S(2)}, u32[]{:S(2)}) collective-permute-start(bf16[32,8,128]{2,1,0:T(8,128)(2,1)} %x_ref.3), channel_id=1, source_target_pairs={{0,1},{1,0},{2,3},{3,2},{4,5},{5,4},{6,7},{7,6},{8,9},{9,8},{10,11... | collective-permute-start | bytes 196616 | tf_op jit(solution)/shard_map/ppermute | solution.py:151
  5.5 0.0 copy-start
  5.5 0.8 %copy-done = bf16[32,8,128]{2,1,0:T(8,128)(2,1)S(1)} copy-done((bf16[32,8,128]{2,1,0:T(8,128)(2,1)S(1)}, bf16[32,8,128]{2,1,0:T(8,128)(2,1)}, u32[]{:S(2)}) %copy-start) | copy-done | bytes 65560
  6.4 0.1 edges.1
  6.4 3.8 %collective-permute-start.2 = (bf16[32,128]{1,0:T(8,128)(2,1)S(1)}, bf16[32,128]{1,0:T(8,128)(2,1)S(1)}, u32[]{:S(2)}, u32[]{:S(2)}) collective-permute-start(bf16[32,128]{1,0:T(8,128)(2,1)S(1)} %get-tuple-element.17), channel_id=1, source_target_pairs={{0,8},{8,0},{16,24},{24,16},{32,40},{40,32},{48,56},{56,48},{64,72... | collective-permute-start | bytes 24584 | tf_op jit(solution)/shard_map/ppermute | solution.py:162
  10.2 18.0 %collective-permute-start.3 = (bf16[32,128]{1,0:T(8,128)(2,1)S(1)}, bf16[32,128]{1,0:T(8,128)(2,1)S(1)}, u32[]{:S(2)}, u32[]{:S(2)}) collective-permute-start(bf16[32,128]{1,0:T(8,128)(2,1)S(1)} %get-tuple-element.18), channel_id=1, source_target_pairs={{8,16},{16,8},{24,32},{32,24},{40,48},{48,40},{56,64},{64,56},{72,... | collective-permute-start | bytes 24584 | tf_op jit(solution)/shard_map/ppermute | solution.py:163
  28.9 0.7 %add_bitcast_fusion = s32[32]{0:T(128)S(1)} fusion(s32[1,1,32]{2,1,0:T(1,128)} %param.7, s32[1,1,32]{2,1,0:T(1,128)} %param.8), kind=kLoop, calls=%fused_computation.1 | loop fusion | flops 64 | bytes 384 | tf_op jit(solution)/shard_map/add | solution.py:150
  29.6 0.1 pad_add_fusion.info_ref
  29.7 2.0 %inner.1 = (f32[129,32,128]{2,1,0:T(8,128)S(1)}, bf16[32,384,128]{2,1,0:T(8,128)(2,1)S(1)}) custom-call(s32[33]{0:T(128)S(1)} %pad_add_fusion.info_ref, bf16[32,8,128]{2,1,0:T(8,128)(2,1)S(1)} %copy-done, bf16[32,384,128]{2,1,0:T(8,128)(2,1)} %bitcast.5), custom_call_target="tpu_custom_call" | custom-call | flops 100000000 | bytes 6000000 | tf_op jit(solution)/shard_map/inner/pallas_call | solution.py:166
  31.7 0.0 collective-permute-done.2.near_ref
  31.7 0.0 collective-permute-done.3.far_ref
  31.7 0.0 collective-permute-done.1.beside_ref
  31.7 0.0 collective-permute-done.pair_ref
  31.7 1.0 %border.1 = (f32[129,32,128]{2,1,0:T(8,128)S(1)}, bf16[64,32,128]{2,1,0:T(8,128)(2,1)S(1)}) custom-call(s32[33]{0:T(128)S(1)} %pad_add_fusion.info_ref, bf16[32,8,128]{2,1,0:T(8,128)(2,1)S(1)} %collective-permute-done.pair_ref, bf16[32,8,128]{2,1,0:T(8,128)(2,1)S(1)} %collective-permute-done.1.beside_ref, ...), custom_call_target="tpu_custom_call", output_to_operand_aliasing={{0}: (6, {})} | custom-call | tf_op jit(solution)/shard_map/border/pallas_call | solution.py:180
  32.7 1.9 %collective-permute-start.4 = (bf16[64,32,128]{2,1,0:T(8,128)(2,1)S(1)}, bf16[64,32,128]{2,1,0:T(8,128)(2,1)S(1)}, u32[]{:S(2)}, u32[]{:S(2)}) collective-permute-start(bf16[64,32,128]{2,1,0:T(8,128)(2,1)S(1)} %get-tuple-element.22), channel_id=1, source_target_pairs={{0,1},{1,0},{2,3},{3,2},{4,5},{5,4},{6,7},{7,6},{8,9},{9,8},{10,11... | collective-permute-start | bytes 1572872 | tf_op jit(solution)/shard_map/ppermute | solution.py:194
  34.6 1.9 %collective-permute-done.4.got_ref = bf16[64,32,128]{2,1,0:T(8,128)(2,1)S(1)} collective-permute-done((bf16[64,32,128]{2,1,0:T(8,128)(2,1)S(1)}, bf16[64,32,128]{2,1,0:T(8,128)(2,1)S(1)}, u32[]{:S(2)}, u32[]{:S(2)}) %collective-permute-start.4) | collective-permute-done | bytes 524320 | tf_op jit(solution)/shard_map/ppermute | solution.py:194
  36.5 0.1 pair_sum.1
  36.6 5.3 %collective-permute-start.5 = (bf16[16,32,128]{2,1,0:T(8,128)(2,1)S(1)}, bf16[16,32,128]{2,1,0:T(8,128)(2,1)S(1)}, u32[]{:S(2)}, u32[]{:S(2)}) collective-permute-start(bf16[16,32,128]{2,1,0:T(8,128)(2,1)S(1)} %get-tuple-element.24), channel_id=1, source_target_pairs={{0,4},{1,5},{2,6},{3,7},{4,0},{5,1},{6,2},{7,3},{8,12},{9,13},{10,... | collective-permute-start | bytes 393224 | tf_op jit(solution)/shard_map/ppermute | solution.py:204
  41.9 1.9 %collective-permute-start.6 = (bf16[16,32,128]{2,1,0:T(8,128)(2,1)S(1)}, bf16[16,32,128]{2,1,0:T(8,128)(2,1)S(1)}, u32[]{:S(2)}, u32[]{:S(2)}) collective-permute-start(bf16[16,32,128]{2,1,0:T(8,128)(2,1)S(1)} %get-tuple-element.25), channel_id=1, source_target_pairs={{0,2},{1,3},{2,0},{3,1},{4,6},{5,7},{6,4},{7,5},{8,10},{9,11},{10,... | collective-permute-start | bytes 393224 | tf_op jit(solution)/shard_map/ppermute | solution.py:204
  43.8 3.3 %collective-permute-start.7 = (bf16[16,32,128]{2,1,0:T(8,128)(2,1)S(1)}, bf16[16,32,128]{2,1,0:T(8,128)(2,1)S(1)}, u32[]{:S(2)}, u32[]{:S(2)}) collective-permute-start(bf16[16,32,128]{2,1,0:T(8,128)(2,1)S(1)} %get-tuple-element.26), channel_id=1, source_target_pairs={{0,6},{1,7},{2,4},{3,5},{4,2},{5,3},{6,0},{7,1},{8,14},{9,15},{10,... | collective-permute-start | bytes 393224 | tf_op jit(solution)/shard_map/ppermute | solution.py:204
  47.1 0.0 collective-permute-done.5.refs_0_
  47.1 2.0 %collective-permute-done.6.refs_1_ = bf16[16,32,128]{2,1,0:T(8,128)(2,1)S(1)} collective-permute-done((bf16[16,32,128]{2,1,0:T(8,128)(2,1)S(1)}, bf16[16,32,128]{2,1,0:T(8,128)(2,1)S(1)}, u32[]{:S(2)}, u32[]{:S(2)}) %collective-permute-start.6) | collective-permute-done | bytes 131104 | tf_op jit(solution)/shard_map/ppermute | solution.py:204
  49.1 3.1 %collective-permute-done.7.refs_2_ = bf16[16,32,128]{2,1,0:T(8,128)(2,1)S(1)} collective-permute-done((bf16[16,32,128]{2,1,0:T(8,128)(2,1)S(1)}, bf16[16,32,128]{2,1,0:T(8,128)(2,1)S(1)}, u32[]{:S(2)}, u32[]{:S(2)}) %collective-permute-start.7) | collective-permute-done | bytes 131104 | tf_op jit(solution)/shard_map/ppermute | solution.py:204
  52.2 0.1 total.1
  52.3 1.9 %collective-permute-start.8 = (bf16[8,32,128]{2,1,0:T(8,128)(2,1)S(1)}, bf16[8,32,128]{2,1,0:T(8,128)(2,1)S(1)}, u32[]{:S(2)}, u32[]{:S(2)}) collective-permute-start(bf16[8,32,128]{2,1,0:T(8,128)(2,1)S(1)} %get-tuple-element.28), channel_id=1, source_target_pairs={{0,8},{8,16},{16,24},{24,32},{32,40},{40,48},{48,56},{56,64},{64,7... | collective-permute-start | bytes 196616 | tf_op jit(solution)/shard_map/ppermute | solution.py:216
  54.2 6.3 %collective-permute-done.8.got_ref = bf16[8,32,128]{2,1,0:T(8,128)(2,1)S(1)} collective-permute-done((bf16[8,32,128]{2,1,0:T(8,128)(2,1)S(1)}, bf16[8,32,128]{2,1,0:T(8,128)(2,1)S(1)}, u32[]{:S(2)}, u32[]{:S(2)}) %collective-permute-start.8) | collective-permute-done | bytes 65568 | tf_op jit(solution)/shard_map/ppermute | solution.py:216
  60.5 0.7 %final.1 = f32[32,1024]{1,0:T(8,128)} custom-call(f32[8,32,128]{2,1,0:T(8,128)S(1)} %get-tuple-element.27.here_ref, bf16[8,32,128]{2,1,0:T(8,128)(2,1)S(1)} %collective-permute-done.8.got_ref), custom_call_target="tpu_custom_call" | custom-call | tf_op jit(solution)/shard_map/final/pallas_call | solution.py:217
Async XLA Ops:
  0.0 31.7 %collective-permute-start.1 = (bf16[32,8,128]{2,1,0:T(8,128)(2,1)}, bf16[32,8,128]{2,1,0:T(8,128)(2,1)S(1)}, u32[]{:S(2)}, u32[]{:S(2)}) collective-permute-start(bf16[32,8,128]{2,1,0:T(8,128)(2,1)} %x_ref.3), channel_id=1, source_target_pairs={{1,2},{2,1},{3,4},{4,3},{5,6},{6,5},{9,10},{10,9},{11,12},{12,11},... | collective-permute-start | bytes 196616 | tf_op jit(solution)/shard_map/ppermute | solution.py:152
  0.7 31.1 %collective-permute-start = (bf16[32,8,128]{2,1,0:T(8,128)(2,1)}, bf16[32,8,128]{2,1,0:T(8,128)(2,1)S(1)}, u32[]{:S(2)}, u32[]{:S(2)}) collective-permute-start(bf16[32,8,128]{2,1,0:T(8,128)(2,1)} %x_ref.3), channel_id=1, source_target_pairs={{0,1},{1,0},{2,3},{3,2},{4,5},{5,4},{6,7},{7,6},{8,9},{9,8},{10,11... | collective-permute-start | bytes 196616 | tf_op jit(solution)/shard_map/ppermute | solution.py:151
  5.5 0.8 %copy-start = (bf16[32,8,128]{2,1,0:T(8,128)(2,1)S(1)}, bf16[32,8,128]{2,1,0:T(8,128)(2,1)}, u32[]{:S(2)}) copy-start(bf16[32,8,128]{2,1,0:T(8,128)(2,1)} %x_ref.3) | copy-start | bytes 196612
  6.4 25.3 %collective-permute-start.2 = (bf16[32,128]{1,0:T(8,128)(2,1)S(1)}, bf16[32,128]{1,0:T(8,128)(2,1)S(1)}, u32[]{:S(2)}, u32[]{:S(2)}) collective-permute-start(bf16[32,128]{1,0:T(8,128)(2,1)S(1)} %get-tuple-element.17), channel_id=1, source_target_pairs={{0,8},{8,0},{16,24},{24,16},{32,40},{40,32},{48,56},{56,48},{64,72... | collective-permute-start | bytes 24584 | tf_op jit(solution)/shard_map/ppermute | solution.py:162
  10.2 21.4 %collective-permute-start.3 = (bf16[32,128]{1,0:T(8,128)(2,1)S(1)}, bf16[32,128]{1,0:T(8,128)(2,1)S(1)}, u32[]{:S(2)}, u32[]{:S(2)}) collective-permute-start(bf16[32,128]{1,0:T(8,128)(2,1)S(1)} %get-tuple-element.18), channel_id=1, source_target_pairs={{8,16},{16,8},{24,32},{32,24},{40,48},{48,40},{56,64},{64,56},{72,... | collective-permute-start | bytes 24584 | tf_op jit(solution)/shard_map/ppermute | solution.py:163
  32.7 3.8 %collective-permute-start.4 = (bf16[64,32,128]{2,1,0:T(8,128)(2,1)S(1)}, bf16[64,32,128]{2,1,0:T(8,128)(2,1)S(1)}, u32[]{:S(2)}, u32[]{:S(2)}) collective-permute-start(bf16[64,32,128]{2,1,0:T(8,128)(2,1)S(1)} %get-tuple-element.22), channel_id=1, source_target_pairs={{0,1},{1,0},{2,3},{3,2},{4,5},{5,4},{6,7},{7,6},{8,9},{9,8},{10,11... | collective-permute-start | bytes 1572872 | tf_op jit(solution)/shard_map/ppermute | solution.py:194
  36.6 10.5 %collective-permute-start.5 = (bf16[16,32,128]{2,1,0:T(8,128)(2,1)S(1)}, bf16[16,32,128]{2,1,0:T(8,128)(2,1)S(1)}, u32[]{:S(2)}, u32[]{:S(2)}) collective-permute-start(bf16[16,32,128]{2,1,0:T(8,128)(2,1)S(1)} %get-tuple-element.24), channel_id=1, source_target_pairs={{0,4},{1,5},{2,6},{3,7},{4,0},{5,1},{6,2},{7,3},{8,12},{9,13},{10,... | collective-permute-start | bytes 393224 | tf_op jit(solution)/shard_map/ppermute | solution.py:204
  41.9 7.2 %collective-permute-start.6 = (bf16[16,32,128]{2,1,0:T(8,128)(2,1)S(1)}, bf16[16,32,128]{2,1,0:T(8,128)(2,1)S(1)}, u32[]{:S(2)}, u32[]{:S(2)}) collective-permute-start(bf16[16,32,128]{2,1,0:T(8,128)(2,1)S(1)} %get-tuple-element.25), channel_id=1, source_target_pairs={{0,2},{1,3},{2,0},{3,1},{4,6},{5,7},{6,4},{7,5},{8,10},{9,11},{10,... | collective-permute-start | bytes 393224 | tf_op jit(solution)/shard_map/ppermute | solution.py:204
  43.8 8.4 %collective-permute-start.7 = (bf16[16,32,128]{2,1,0:T(8,128)(2,1)S(1)}, bf16[16,32,128]{2,1,0:T(8,128)(2,1)S(1)}, u32[]{:S(2)}, u32[]{:S(2)}) collective-permute-start(bf16[16,32,128]{2,1,0:T(8,128)(2,1)S(1)} %get-tuple-element.26), channel_id=1, source_target_pairs={{0,6},{1,7},{2,4},{3,5},{4,2},{5,3},{6,0},{7,1},{8,14},{9,15},{10,... | collective-permute-start | bytes 393224 | tf_op jit(solution)/shard_map/ppermute | solution.py:204
  52.3 8.3 %collective-permute-start.8 = (bf16[8,32,128]{2,1,0:T(8,128)(2,1)S(1)}, bf16[8,32,128]{2,1,0:T(8,128)(2,1)S(1)}, u32[]{:S(2)}, u32[]{:S(2)}) collective-permute-start(bf16[8,32,128]{2,1,0:T(8,128)(2,1)S(1)} %get-tuple-element.28), channel_id=1, source_target_pairs={{0,8},{8,16},{16,24},{24,32},{32,40},{40,48},{48,56},{56,64},{64,7... | collective-permute-start | bytes 196616 | tf_op jit(solution)/shard_map/ppermute | solution.py:216

commit v3 on v2

v3 whole, which is shorter than its diff:
```python
import jax
import jax.numpy as jnp
from jax import lax
from jax.experimental import pallas as pl
from jax.experimental.pallas import tpu as pltpu
from jax.sharding import PartitionSpec as P

OB_DEV = 8
LANES = 128
GROUP = 8
VMEM = pl.BlockSpec(memory_space=pltpu.VMEM)
SMEM = pl.BlockSpec(memory_space=pltpu.SMEM)
HBM = pl.BlockSpec(memory_space=pltpu.HBM)


def hbm(array):
    return pltpu.with_memory_space_constraint(array, pltpu.HBM)


def swap_pairs(count, first):
    pairs = []
    for i in range(first, count - 1, 2):
        pairs += [(i, i + 1), (i + 1, i)]
    return pairs


def xor_pairs(count, mask):
    return [(i, i ^ mask) for i in range(count)]


def index_copies(refs, scratch, sems):
    return [pltpu.make_async_copy(ref, to, sems.at[i]) for i, (ref, to) in enumerate(zip(refs, scratch))]


def entry(row_ref, code_ref, e, live):
    core, along = lax.axis_index("sub") % 2, lax.axis_index("sub") // 2
    code = code_ref[0, 0, e]
    dest = code // 16
    slot = ((dest % 2) ^ core) * 64 + ((dest // 2) ^ along) * 16 + code % 16
    return row_ref[0, 0, e], jnp.where(e < live, slot, 128)


def inner_kernel(
    row_hbm, code_hbm, live_ref, x_hbm, w_hbm, acc_ref, w_ref,
    row_ref, code_ref, x_ref, xf, source, index_sems, x_sem, sems,
):
    fields, rows, width = x_ref.shape
    flat = fields * rows
    capacity = w_ref.shape[0]
    indices = index_copies((row_hbm, code_hbm), (row_ref, code_ref), index_sems)
    x_copy = pltpu.make_async_copy(x_hbm, x_ref, x_sem)

    def load(start):
        span = pl.ds(start, GROUP)
        return pltpu.make_async_copy(w_hbm.at[span], w_ref.at[span], sems.at[start // GROUP])

    for copy in indices:
        copy.start()
    x_copy.start()
    load(0).start()
    acc_ref[...] = jnp.zeros_like(acc_ref)
    for copy in indices:
        copy.wait()
    live = live_ref[0, 0]
    for start in range(GROUP, capacity, GROUP):
        pl.when(start < live)(lambda start=start: load(start).start())
    x_copy.wait()
    x = x_ref[...].astype(jnp.float32).reshape(flat, width)
    lane = lax.broadcasted_iota(jnp.int32, (flat, width), 1)
    later = pltpu.roll(jnp.where(lane == 0, 0.0, x), width - 1, 1)
    earlier = pltpu.roll(jnp.where(lane == width - 1, 0.0, x), 1, 1)
    xf[0] = x
    xf[1] = 0.5 * (later - earlier)

    def row(which, r):
        return xf[which, pl.ds(r, fields, stride=rows), :]

    for r in range(rows):
        up = row(0, r - 1) if r > 0 else 0.0
        down = row(0, r + 1) if r < rows - 1 else 0.0
        source[r, :, 0:width] = row(0, r).astype(jnp.bfloat16)
        source[r, :, width : 2 * width] = row(1, r).astype(jnp.bfloat16)
        source[r, :, 2 * width : 3 * width] = (0.5 * (down - up)).astype(jnp.bfloat16)

    def accumulate(start):
        load(start).wait()
        for e in range(start, start + GROUP):
            r, slot = entry(row_ref, code_ref, e, live)
            acc_ref[slot] += jnp.dot(source[r], w_ref[e], preferred_element_type=jnp.float32)

    accumulate(0)
    for start in range(GROUP, capacity, GROUP):
        pl.when(start < live)(lambda start=start: accumulate(start))


def border_kernel(
    row_hbm, code_hbm, live_ref, beside_ref, near_ref, far_ref, pair_ref, w_ref, acc_in, acc_ref, send_ref,
    row_ref, code_ref, xf, side, ends, index_sems,
):
    del acc_in
    fields, rows, width = pair_ref.shape
    flat = fields * rows
    capacity = w_ref.shape[0]
    indices = index_copies((row_hbm, code_hbm), (row_ref, code_ref), index_sems)
    for copy in indices:
        copy.start()
    odd_sub, odd_band = lax.axis_index("sub") % 2 == 1, lax.axis_index("band") % 2 == 1
    pair, beside, near, far = (
        ref[...].astype(jnp.float32).reshape(flat, width) for ref in (pair_ref, beside_ref, near_ref, far_ref)
    )
    left = jnp.where(odd_sub, pair, beside)[:, width - 1 : width]
    right = jnp.where(odd_sub, beside, pair)[:, 0:1]
    xf[0] = jnp.broadcast_to(-0.5 * left, (flat, width))
    xf[1] = jnp.broadcast_to(0.5 * right, (flat, width))
    xf[2] = -0.5 * jnp.where(odd_band, near, far)
    xf[3] = 0.5 * jnp.where(odd_band, far, near)

    def row(which, r):
        return xf[which, pl.ds(r, fields, stride=rows), :]

    for r in range(rows):
        for which in range(2):
            side[which, r] = row(which, r)
    ends[...] = jnp.zeros_like(ends)
    ends[0] = row(2, rows - 1).astype(jnp.bfloat16)
    ends[rows - 1] = row(3, 0).astype(jnp.bfloat16)
    for copy in indices:
        copy.wait()
    live = live_ref[0, 0]

    def accumulate(start):
        for e in range(start, start + GROUP):
            r, slot = entry(row_ref, code_ref, e, live)
            first = w_ref[e, width : width + 16, :].astype(jnp.float32)[0:1]
            last = w_ref[e, 2 * width - 16 : 2 * width, :].astype(jnp.float32)[15:16]
            acc_ref[slot] += (
                jnp.dot(ends[r], w_ref[e, 2 * width : 3 * width, :], preferred_element_type=jnp.float32)
                + side[0, r] * first
                + side[1, r] * last
            )

    accumulate(0)
    for start in range(GROUP, capacity, GROUP):
        pl.when(start < live)(lambda start=start: accumulate(start))
    half = send_ref.shape[0]
    send_ref[...] = acc_ref[half : 2 * half].astype(jnp.bfloat16)


def pair_sum_kernel(keep_ref, got_ref, own_ref, out_ref):
    along = lax.axis_index("sub") // 2
    chips, count = out_ref.shape[:2]
    for k in range(chips):
        span = slice(k * count, (k + 1) * count)
        out_ref[along ^ k] = (keep_ref[span] + got_ref[span].astype(jnp.float32)).astype(jnp.bfloat16)
    own_ref[...] = keep_ref[0:count] + got_ref[0:count].astype(jnp.float32)


def total_kernel(own_ref, got_ref, here_ref, next_ref):
    along = lax.axis_index("sub") // 2
    total = own_ref[...]
    for k in range(1, got_ref.shape[0]):
        total = total + got_ref[along ^ k].astype(jnp.float32)
    here_ref[...] = total[:OB_DEV]
    next_ref[...] = total[OB_DEV:].astype(jnp.bfloat16)


def final_kernel(here_ref, got_ref, out_ref):
    for q in range(OB_DEV):
        out_ref[:, q * LANES : (q + 1) * LANES] = here_ref[q] + got_ref[q].astype(jnp.float32)


def shards(atmos_flux, weight_tiles, source_row, target_code, live_count):
    fields, rows, width = atmos_flux.shape
    capacity = weight_tiles.shape[2]
    subs, bands = lax.axis_size("sub"), lax.axis_size("band")
    blocks = 2 * OB_DEV
    half = subs // 2 * blocks
    params = pltpu.CompilerParams(vmem_limit_bytes=24 * 2**20)
    far = lax.ppermute(atmos_flux, "band", swap_pairs(bands, 1))
    beside = lax.ppermute(atmos_flux, "sub", swap_pairs(subs, 1))
    pair = lax.ppermute(atmos_flux, "sub", swap_pairs(subs, 0))
    near = lax.ppermute(atmos_flux, "band", swap_pairs(bands, 0))
    sums = jax.ShapeDtypeStruct((2 * half + 1, fields, width), jnp.float32)
    indices = (hbm(source_row), hbm(target_code))
    index_scratch = [pltpu.SMEM(a.shape, a.dtype) for a in indices]
    tiles = hbm(weight_tiles[0, 0])
    acc, held = pl.pallas_call(
        inner_kernel,
        out_shape=(sums, jax.ShapeDtypeStruct(tiles.shape, tiles.dtype)),
        in_specs=[HBM, HBM, SMEM, HBM, HBM],
        out_specs=(VMEM, VMEM),
        scratch_shapes=index_scratch + [
            pltpu.VMEM((fields, rows, width), atmos_flux.dtype),
            pltpu.VMEM((2, fields * rows, width), jnp.float32),
            pltpu.VMEM((rows, fields, 3 * width), jnp.bfloat16),
            pltpu.SemaphoreType.DMA((2,)),
            pltpu.SemaphoreType.DMA,
            pltpu.SemaphoreType.DMA((capacity // GROUP,)),
        ],
        compiler_params=params,
        cost_estimate=pl.CostEstimate(flops=100_000_000, bytes_accessed=6_000_000, transcendentals=0),
        name="inner",
    )(*indices, live_count, hbm(atmos_flux), tiles)
    acc, send = pl.pallas_call(
        border_kernel,
        out_shape=(sums, jax.ShapeDtypeStruct((half, fields, width), jnp.bfloat16)),
        in_specs=[HBM, HBM, SMEM] + [VMEM] * 6,
        out_specs=(VMEM, VMEM),
        scratch_shapes=index_scratch + [
            pltpu.VMEM((4, fields * rows, width), jnp.float32),
            pltpu.VMEM((2, rows, fields, width), jnp.float32),
            pltpu.VMEM((rows, fields, width), jnp.bfloat16),
            pltpu.SemaphoreType.DMA((2,)),
        ],
        input_output_aliases={8: 0},
        compiler_params=params,
        name="border",
    )(*indices, live_count, beside, near, far, pair, held, acc)
    got = lax.ppermute(send, "sub", xor_pairs(subs, 1))
    own, outs = pl.pallas_call(
        pair_sum_kernel,
        out_shape=(
            jax.ShapeDtypeStruct((blocks, fields, width), jnp.float32),
            jax.ShapeDtypeStruct((subs // 2, blocks, fields, width), jnp.bfloat16),
        ),
        in_specs=[VMEM] * 2,
        out_specs=(VMEM, VMEM),
        compiler_params=params,
        name="pair_sum",
    )(acc, got)
    groups = [list(range(core, subs, 2)) for core in range(2)]
    arrived = lax.all_to_all(outs, "sub", split_axis=0, concat_axis=0, axis_index_groups=groups, tiled=True)
    here, ahead = pl.pallas_call(
        total_kernel,
        out_shape=(
            jax.ShapeDtypeStruct((OB_DEV, fields, width), jnp.float32),
            jax.ShapeDtypeStruct((OB_DEV, fields, width), jnp.bfloat16),
        ),
        in_specs=[VMEM] * 2,
        out_specs=(VMEM, VMEM),
        compiler_params=params,
        name="total",
    )(own, arrived)
    behind = lax.ppermute(ahead, "band", [(i, (i + 1) % bands) for i in range(bands)])
    return pl.pallas_call(
        final_kernel,
        out_shape=jax.ShapeDtypeStruct((fields, OB_DEV * width), jnp.float32),
        in_specs=[VMEM] * 2,
        out_specs=VMEM,
        compiler_params=params,
        name="final",
    )(here, behind)


def solution(mesh):
    return jax.shard_map(
        shards,
        mesh=mesh,
        in_specs=(
            P(None, "band", "sub"),
            P("band", "sub", None, None, None),
            P("band", "sub", None),
            P("band", "sub", None),
            P("band", "sub"),
        ),
        out_specs=P(None, ("band", "sub")),
        check_vma=False,
    )
```

time: 61.6 us -> 57.9 us (0.940)
  blocking collectives: 0 us -> 13.7 us
  starting transfers between devices: 41.6 us -> 32.2 us
  waiting for transfers between devices: 13.3 us -> 6.22 us
  local copies, waits for them, and re-layouts: 0.83 us -> 0 us
  other arithmetic: 0.75 us -> 0 us
    all_to_all x0 -> x1, blocking collectives: none -> 13.7 us  [shards(): lax.all_to_all(outs, 'sub', split_axis=0, concat_axis=0, axis_index_group...]
    ppermute x5 -> x2, starting transfers between devices: 32.3 us -> 20.9 us  [the longest x1 18.9 us: shards(): far = lax.ppermute(atmos_flux, 'band', swap_pairs(bands, 1))]
    ppermute x5 -> x2, waiting for transfers between devices: 5.1 us -> 0.01 us  [the longest x1 0.01 us: shards(): far = lax.ppermute(atmos_flux, 'band', swap_pairs(bands, 1))]
    ppermute x1, starting transfers between devices: 1.92 us -> 3.92 us  [shards(): lax.ppermute(ahead, 'band', [(i, (i + 1) % bands) for i in range(bands)])]
    ppermute x1, waiting for transfers between devices: 6.34 us -> 4.34 us  [shards(): lax.ppermute(ahead, 'band', [(i, (i + 1) % bands) for i in range(bands)])]
    unnamed x2 -> x0, local copies, waits for them, and re-layouts: 0.83 us -> none
    add x1 -> x0, other arithmetic: 0.68 us -> none  [shards(): source_row[0, 0] + 8 * target_code[0, 0]]
  transfers between devices with their start and end apart: 9 -> 6, of which waited for: 4 -> 2; matrix products, arithmetic and copies ran while one was open for 1% -> 0% of each run, Pallas kernels for 3% -> 4%
where the time goes in v3:
time: 57.9 us; the launch traced here: 57.1 us
  starting transfers between devices  32.2 us (56%)
  blocking collectives  13.7 us (24%)
  waiting for transfers between devices  6.22 us (11%)
  Pallas kernels  4.19 us (7%)
  between operations  0.75 us (1%)
    ppermute x1, starting transfers between devices, shards(): far = lax.ppermute(atmos_flux, 'band', swap_pairs(bands, 1))  18.9 us
    all_to_all x1, blocking collectives, shards(): lax.all_to_all(outs, 'sub', split_axis=0, concat_axis=0, axis_index_group...  13.7 us
    ppermute x1, starting transfers between devices, shards(): pair = lax.ppermute(atmos_flux, 'sub', swap_pairs(subs, 0))  4.84 us
    ppermute x1, waiting for transfers between devices, shards(): lax.ppermute(ahead, 'band', [(i, (i + 1) % bands) for i in range(bands)])  4.34 us
    ppermute x1, starting transfers between devices, shards(): lax.ppermute(ahead, 'band', [(i, (i + 1) % bands) for i in range(bands)])  3.92 us
    pallas_call x1, Pallas kernels, shards(): pl.pallas_call(inner_kernel, out_shape=(sums, jax.ShapeDtypeStruct(tiles....  2.2 us
    ppermute x1, starting transfers between devices, shards(): got = lax.ppermute(send, 'sub', xor_pairs(subs, 1))  1.92 us
    ppermute x1, starting transfers between devices, shards(): near = lax.ppermute(atmos_flux, 'band', swap_pairs(bands, 0))  1.92 us
  transfers between devices with their start and end apart: 6, of which 2 were waited for; matrix products, arithmetic and copies ran while one was open for 0% of the time, Pallas kernels for 4%

profile of v3, /device:TPU:6, one launch (start us, length us, event | category | flops | bytes accessed | tf_op | source)
XLA Modules:
  0.0 57.1 jit_solution(5717180857430958777)
XLA Ops:
  0.0 18.9 %collective-permute-start.2 = (bf16[32,8,128]{2,1,0:T(8,128)(2,1)}, bf16[32,8,128]{2,1,0:T(8,128)(2,1)S(1)}, u32[]{:S(2)}, u32[]{:S(2)}) collective-permute-start(bf16[32,8,128]{2,1,0:T(8,128)(2,1)} %x_hbm.1), channel_id=1, source_target_pairs={{8,16},{16,8},{24,32},{32,24},{40,48},{48,40},{56,64},{64,56},{72,... | collective-permute-start | bytes 196616 | tf_op jit(solution)/shard_map/ppermute | solution.py:179
  18.9 1.9 %collective-permute-start.1 = (bf16[32,8,128]{2,1,0:T(8,128)(2,1)}, bf16[32,8,128]{2,1,0:T(8,128)(2,1)S(1)}, u32[]{:S(2)}, u32[]{:S(2)}) collective-permute-start(bf16[32,8,128]{2,1,0:T(8,128)(2,1)} %x_hbm.1), channel_id=1, source_target_pairs={{0,8},{8,0},{16,24},{24,16},{32,40},{40,32},{48,56},{56,48},{64,72... | collective-permute-start | bytes 196616 | tf_op jit(solution)/shard_map/ppermute | solution.py:182
  20.9 0.7 %collective-permute-start = (bf16[32,8,128]{2,1,0:T(8,128)(2,1)}, bf16[32,8,128]{2,1,0:T(8,128)(2,1)S(1)}, u32[]{:S(2)}, u32[]{:S(2)}) collective-permute-start(bf16[32,8,128]{2,1,0:T(8,128)(2,1)} %x_hbm.1), channel_id=1, source_target_pairs={{1,2},{2,1},{3,4},{4,3},{5,6},{6,5},{9,10},{10,9},{11,12},{12,11},... | collective-permute-start | bytes 196616 | tf_op jit(solution)/shard_map/ppermute | solution.py:180
  21.5 4.8 %collective-permute-start.3 = (bf16[32,8,128]{2,1,0:T(8,128)(2,1)}, bf16[32,8,128]{2,1,0:T(8,128)(2,1)S(1)}, u32[]{:S(2)}, u32[]{:S(2)}) collective-permute-start(bf16[32,8,128]{2,1,0:T(8,128)(2,1)} %x_hbm.1), channel_id=1, source_target_pairs={{0,1},{1,0},{2,3},{3,2},{4,5},{5,4},{6,7},{7,6},{8,9},{9,8},{10,11... | collective-permute-start | bytes 196616 | tf_op jit(solution)/shard_map/ppermute | solution.py:181
  27.0 2.2 %inner.1 = (f32[129,32,128]{2,1,0:T(8,128)S(1)}, bf16[32,384,128]{2,1,0:T(8,128)(2,1)S(1)}) custom-call(s32[1,1,32]{2,1,0:T(1,128)} %row_hbm.3, s32[1,1,32]{2,1,0:T(1,128)} %code_hbm.3, s32[1,1]{1,0:T(1,128)S(6)} %copy.8.live_ref, bf16[32,8,128]{2,1,0:T(8,128)(2,1)} %x_hbm.1, bf16[32,384,128]{2,1,0:T(8,128)(2,1)} %bitcast.1), custom_call_target="tpu_custom_call" | custom-call | flops 100000000 | bytes 6000000 | tf_op jit(solution)/shard_map/inner/pallas_call | solution.py:187
  29.2 0.0 collective-permute-done.2.far_ref
  29.3 0.0 collective-permute-done.1.near_ref
  29.3 0.0 collective-permute-done.beside_ref
  29.3 0.0 collective-permute-done.3.pair_ref
  29.3 1.2 %border.1 = (f32[129,32,128]{2,1,0:T(8,128)S(1)}, bf16[64,32,128]{2,1,0:T(8,128)(2,1)S(1)}) custom-call(s32[1,1,32]{2,1,0:T(1,128)} %row_hbm.3, s32[1,1,32]{2,1,0:T(1,128)} %code_hbm.3, s32[1,1]{1,0:T(1,128)S(6)} %copy.8.live_ref, bf16[32,8,128]{2,1,0:T(8,128)(2,1)S(1)} %collective-permute-done.beside_ref, ...), custom_call_target="tpu_custom_call", output_to_operand_aliasing={{0}: (8, {})} | custom-call | tf_op jit(solution)/shard_map/border/pallas_call | solution.py:204
  30.5 1.9 %collective-permute-start.4 = (bf16[64,32,128]{2,1,0:T(8,128)(2,1)S(1)}, bf16[64,32,128]{2,1,0:T(8,128)(2,1)S(1)}, u32[]{:S(2)}, u32[]{:S(2)}) collective-permute-start(bf16[64,32,128]{2,1,0:T(8,128)(2,1)S(1)} %get-tuple-element.16), channel_id=1, source_target_pairs={{0,1},{1,0},{2,3},{3,2},{4,5},{5,4},{6,7},{7,6},{8,9},{9,8},{10,11... | collective-permute-start | bytes 1572872 | tf_op jit(solution)/shard_map/ppermute | solution.py:219
  32.4 1.9 %collective-permute-done.4.got_ref = bf16[64,32,128]{2,1,0:T(8,128)(2,1)S(1)} collective-permute-done((bf16[64,32,128]{2,1,0:T(8,128)(2,1)S(1)}, bf16[64,32,128]{2,1,0:T(8,128)(2,1)S(1)}, u32[]{:S(2)}, u32[]{:S(2)}) %collective-permute-start.4) | collective-permute-done | bytes 524320 | tf_op jit(solution)/shard_map/ppermute | solution.py:219
  34.3 0.1 pair_sum.1
  34.4 13.7 %all_to_all.5.got_ref = bf16[4,16,32,128]{3,2,1,0:T(8,128)(2,1)S(1)} all-to-all(bf16[4,16,32,128]{3,2,1,0:T(8,128)(2,1)S(1)} %get-tuple-element.18), channel_id=1, replica_groups={{0,2,4,6},{1,3,5,7},{8,10,12,14},{9,11,13,15},{16,18,20,22},{17,19,21,2..., dimensions={0} | all-to-all | bytes 1048576 | tf_op jit(solution)/shard_map/all_to_all | solution.py:232
  48.1 0.1 total.1
  48.2 3.9 %collective-permute-start.5 = (bf16[8,32,128]{2,1,0:T(8,128)(2,1)S(1)}, bf16[8,32,128]{2,1,0:T(8,128)(2,1)S(1)}, u32[]{:S(2)}, u32[]{:S(2)}) collective-permute-start(bf16[8,32,128]{2,1,0:T(8,128)(2,1)S(1)} %get-tuple-element.20), channel_id=1, source_target_pairs={{0,8},{8,16},{16,24},{24,32},{32,40},{40,48},{48,56},{56,64},{64,7... | collective-permute-start | bytes 196616 | tf_op jit(solution)/shard_map/ppermute | solution.py:244
  52.1 4.3 %collective-permute-done.5.got_ref = bf16[8,32,128]{2,1,0:T(8,128)(2,1)S(1)} collective-permute-done((bf16[8,32,128]{2,1,0:T(8,128)(2,1)S(1)}, bf16[8,32,128]{2,1,0:T(8,128)(2,1)S(1)}, u32[]{:S(2)}, u32[]{:S(2)}) %collective-permute-start.5) | collective-permute-done | bytes 65568 | tf_op jit(solution)/shard_map/ppermute | solution.py:244
  56.4 0.7 %final.1 = f32[32,1024]{1,0:T(8,128)} custom-call(f32[8,32,128]{2,1,0:T(8,128)S(1)} %get-tuple-element.19.here_ref, bf16[8,32,128]{2,1,0:T(8,128)(2,1)S(1)} %collective-permute-done.5.got_ref), custom_call_target="tpu_custom_call" | custom-call | tf_op jit(solution)/shard_map/final/pallas_call | solution.py:245
Async XLA Ops:
  0.0 29.2 %collective-permute-start.2 = (bf16[32,8,128]{2,1,0:T(8,128)(2,1)}, bf16[32,8,128]{2,1,0:T(8,128)(2,1)S(1)}, u32[]{:S(2)}, u32[]{:S(2)}) collective-permute-start(bf16[32,8,128]{2,1,0:T(8,128)(2,1)} %x_hbm.1), channel_id=1, source_target_pairs={{8,16},{16,8},{24,32},{32,24},{40,48},{48,40},{56,64},{64,56},{72,... | collective-permute-start | bytes 196616 | tf_op jit(solution)/shard_map/ppermute | solution.py:179
  18.9 10.3 %collective-permute-start.1 = (bf16[32,8,128]{2,1,0:T(8,128)(2,1)}, bf16[32,8,128]{2,1,0:T(8,128)(2,1)S(1)}, u32[]{:S(2)}, u32[]{:S(2)}) collective-permute-start(bf16[32,8,128]{2,1,0:T(8,128)(2,1)} %x_hbm.1), channel_id=1, source_target_pairs={{0,8},{8,0},{16,24},{24,16},{32,40},{40,32},{48,56},{56,48},{64,72... | collective-permute-start | bytes 196616 | tf_op jit(solution)/shard_map/ppermute | solution.py:182
  20.9 8.4 %collective-permute-start = (bf16[32,8,128]{2,1,0:T(8,128)(2,1)}, bf16[32,8,128]{2,1,0:T(8,128)(2,1)S(1)}, u32[]{:S(2)}, u32[]{:S(2)}) collective-permute-start(bf16[32,8,128]{2,1,0:T(8,128)(2,1)} %x_hbm.1), channel_id=1, source_target_pairs={{1,2},{2,1},{3,4},{4,3},{5,6},{6,5},{9,10},{10,9},{11,12},{12,11},... | collective-permute-start | bytes 196616 | tf_op jit(solution)/shard_map/ppermute | solution.py:180
  21.5 7.7 %collective-permute-start.3 = (bf16[32,8,128]{2,1,0:T(8,128)(2,1)}, bf16[32,8,128]{2,1,0:T(8,128)(2,1)S(1)}, u32[]{:S(2)}, u32[]{:S(2)}) collective-permute-start(bf16[32,8,128]{2,1,0:T(8,128)(2,1)} %x_hbm.1), channel_id=1, source_target_pairs={{0,1},{1,0},{2,3},{3,2},{4,5},{5,4},{6,7},{7,6},{8,9},{9,8},{10,11... | collective-permute-start | bytes 196616 | tf_op jit(solution)/shard_map/ppermute | solution.py:181
  30.5 3.8 %collective-permute-start.4 = (bf16[64,32,128]{2,1,0:T(8,128)(2,1)S(1)}, bf16[64,32,128]{2,1,0:T(8,128)(2,1)S(1)}, u32[]{:S(2)}, u32[]{:S(2)}) collective-permute-start(bf16[64,32,128]{2,1,0:T(8,128)(2,1)S(1)} %get-tuple-element.16), channel_id=1, source_target_pairs={{0,1},{1,0},{2,3},{3,2},{4,5},{5,4},{6,7},{7,6},{8,9},{9,8},{10,11... | collective-permute-start | bytes 1572872 | tf_op jit(solution)/shard_map/ppermute | solution.py:219
  48.2 8.3 %collective-permute-start.5 = (bf16[8,32,128]{2,1,0:T(8,128)(2,1)S(1)}, bf16[8,32,128]{2,1,0:T(8,128)(2,1)S(1)}, u32[]{:S(2)}, u32[]{:S(2)}) collective-permute-start(bf16[8,32,128]{2,1,0:T(8,128)(2,1)S(1)} %get-tuple-element.20), channel_id=1, source_target_pairs={{0,8},{8,16},{16,24},{24,32},{32,40},{40,48},{48,56},{56,64},{64,7... | collective-permute-start | bytes 196616 | tf_op jit(solution)/shard_map/ppermute | solution.py:244

commit v4 on v3

v4 whole, which is shorter than its diff:
```python
import jax
import jax.numpy as jnp
from jax import lax
from jax.experimental import pallas as pl
from jax.experimental.pallas import tpu as pltpu
from jax.sharding import PartitionSpec as P

OB_DEV = 8
PLANE = 32
OUTER = 64
LANES = 128
GROUP = 8
VMEM = pl.BlockSpec(memory_space=pltpu.VMEM)
SMEM = pl.BlockSpec(memory_space=pltpu.SMEM)
HBM = pl.BlockSpec(memory_space=pltpu.HBM)


def hbm(array):
    return pltpu.with_memory_space_constraint(array, pltpu.HBM)


def swap_pairs(count, first):
    pairs = []
    for i in range(first, count - 1, 2):
        pairs += [(i, i + 1), (i + 1, i)]
    return pairs


def xor_pairs(count, mask):
    return [(i, i ^ mask) for i in range(count)]


def index_copies(refs, scratch, sems):
    return [pltpu.make_async_copy(ref, to, sems.at[i]) for i, (ref, to) in enumerate(zip(refs, scratch))]


def entry(row_ref, code_ref, e, live):
    core, along = lax.axis_index("sub") % 2, lax.axis_index("sub") // 2
    code = code_ref[0, 0, e]
    dest = code // 16
    slot = ((dest % 2) ^ core) * 64 + ((dest // 2) ^ along) * 16 + code % 16
    return row_ref[0, 0, e], jnp.where(e < live, slot, 128)


def edge_rows(w_ref, e, width, right_first):
    right = w_ref[e, 2 * width - 16 : 2 * width, :].astype(jnp.float32)[15:16]
    left = w_ref[e, width : width + 16, :].astype(jnp.float32)[0:1]
    return jnp.where(right_first, right, left), jnp.where(right_first, left, right)


def column_block(rows, last, offset):
    place = lax.broadcasted_iota(jnp.int32, rows[0].shape, 1)
    block = jnp.zeros_like(rows[0])
    for r, values in enumerate(rows):
        block = jnp.where(place == offset + r, jnp.where(last, values[:, -1:], values[:, 0:1]), block)
    return block


def inner_kernel(
    row_hbm, code_hbm, live_ref, x_hbm, w_hbm, acc_ref, w_ref, meta_ref,
    row_ref, code_ref, row_lanes, code_lanes, x_ref, xf, source, edge, index_sems, x_sem, sems,
):
    fields, rows, width = x_ref.shape
    flat = fields * rows
    capacity = w_ref.shape[0]
    core, along = lax.axis_index("sub") % 2, lax.axis_index("sub") // 2
    indices = index_copies(
        (row_hbm, code_hbm, row_hbm, code_hbm), (row_ref, code_ref, row_lanes, code_lanes), index_sems
    )
    x_copy = pltpu.make_async_copy(x_hbm, x_ref, x_sem)

    def load(start):
        span = pl.ds(start, GROUP)
        return pltpu.make_async_copy(w_hbm.at[span], w_ref.at[span], sems.at[start // GROUP])

    live = live_ref[0, 0]
    for copy in indices:
        copy.start()
    x_copy.start()
    load(0).start()
    for start in range(GROUP, capacity, GROUP):
        pl.when(start < live)(lambda start=start: load(start).start())
    acc_ref[...] = jnp.zeros_like(acc_ref)
    edge[...] = jnp.zeros_like(edge)
    for copy in indices:
        copy.wait()
    x_copy.wait()
    x = x_ref[...].astype(jnp.float32).reshape(flat, width)
    lane = lax.broadcasted_iota(jnp.int32, (flat, width), 1)
    later = pltpu.roll(jnp.where(lane == 0, 0.0, x), width - 1, 1)
    earlier = pltpu.roll(jnp.where(lane == width - 1, 0.0, x), 1, 1)
    xf[0] = x
    xf[1] = 0.5 * (later - earlier)

    def row(which, r):
        return xf[which, pl.ds(r, fields, stride=rows), :]

    for r in range(rows):
        up = row(0, r - 1) if r > 0 else 0.0
        down = row(0, r + 1) if r < rows - 1 else 0.0
        source[r, :, 0:width] = row(0, r).astype(jnp.bfloat16)
        source[r, :, width : 2 * width] = row(1, r).astype(jnp.bfloat16)
        source[r, :, 2 * width : 3 * width] = (0.5 * (down - up)).astype(jnp.bfloat16)

    def accumulate(start):
        load(start).wait()
        for e in range(start, start + GROUP):
            to_mate, to_side = edge_rows(w_ref, e, width, core == 0)
            edge[0, e : e + 1] = to_mate
            edge[1, e : e + 1] = to_side
        places = [entry(row_ref, code_ref, e, live) for e in range(start, start + GROUP)]
        products = [
            jnp.dot(source[r], w_ref[start + i], preferred_element_type=jnp.float32) for i, (r, _) in enumerate(places)
        ]
        for (_, slot), product in zip(places, products):
            acc_ref[slot] += product

    accumulate(0)
    for start in range(GROUP, capacity, GROUP):
        pl.when(start < live)(lambda start=start: accumulate(start))
    meta_ref[0] = edge[0].astype(jnp.bfloat16)
    meta_ref[3] = edge[1].astype(jnp.bfloat16)
    columns = [row(0, r) for r in range(rows)]
    meta_ref[1] = column_block(columns, core == 0, 0).astype(jnp.bfloat16)
    meta_ref[4] = column_block(columns, core == 1, OUTER + core * rows).astype(jnp.bfloat16)
    code = code_lanes[0]
    dest = code // 16
    slot = ((dest % 2) ^ core) * 64 + ((dest // 2) ^ along) * 16 + code % 16
    alive = lax.broadcasted_iota(jnp.int32, slot.shape, 1) < live
    slot = jnp.where(alive, slot, 128)
    code = jnp.where(alive, code, 255)
    edge[0] = jnp.zeros_like(edge[0])
    edge[0, 0:1, 0:capacity] = row_lanes[0].astype(jnp.float32)
    edge[0, 1:2, 0:capacity] = slot.astype(jnp.float32)
    edge[0, 2:3, 0:capacity] = code.astype(jnp.float32)
    meta_ref[2] = edge[0].astype(jnp.bfloat16)


def border_kernel(
    row_hbm, code_hbm, live_ref, far_ref, first_ref, near_ref, w_ref, meta_ref, acc_in, acc_ref, send_ref,
    row_ref, code_ref, xf, ends, index_sems,
):
    del acc_in
    fields, rows, width = near_ref.shape
    flat = fields * rows
    capacity = w_ref.shape[0]
    indices = index_copies((row_hbm, code_hbm), (row_ref, code_ref), index_sems)
    for copy in indices:
        copy.start()
    odd_band = lax.axis_index("band") % 2 == 1
    near, first, far = (
        ref[...].astype(jnp.float32).reshape(flat, width) for ref in (near_ref, first_ref, far_ref)
    )
    near = near + first
    xf[0] = -0.5 * jnp.where(odd_band, near, far)
    xf[1] = 0.5 * jnp.where(odd_band, far, near)
    ends[...] = jnp.zeros_like(ends)
    ends[0] = xf[0, pl.ds(rows - 1, fields, stride=rows), :].astype(jnp.bfloat16)
    ends[rows - 1] = xf[1, pl.ds(0, fields, stride=rows), :].astype(jnp.bfloat16)
    for copy in indices:
        copy.wait()
    live = live_ref[0, 0]

    def accumulate(start):
        places = [entry(row_ref, code_ref, e, live) for e in range(start, start + GROUP)]
        products = [
            jnp.dot(ends[r], w_ref[start + i, 2 * width : 3 * width, :], preferred_element_type=jnp.float32)
            for i, (r, _) in enumerate(places)
        ]
        for (_, slot), product in zip(places, products):
            acc_ref[slot] += product

    accumulate(0)
    for start in range(GROUP, capacity, GROUP):
        pl.when(start < live)(lambda start=start: accumulate(start))
    extra = meta_ref.shape[0]
    half = send_ref.shape[0] - extra
    send_ref[0:half] = acc_ref[half : 2 * half].astype(jnp.bfloat16)
    send_ref[half : half + extra] = meta_ref[...]


def pair_sum_kernel(keep_ref, sent_ref, got_ref, own_ref, out_ref, select, edges):
    core, along = lax.axis_index("sub") % 2, lax.axis_index("sub") // 2
    count, fields, width = own_ref.shape
    chips = out_ref.shape[0]
    half = chips * count
    lane = lax.broadcasted_iota(jnp.int32, (1, width), 1)
    mine, theirs = sent_ref[half + 2].astype(jnp.float32), got_ref[half + 2].astype(jnp.float32)
    rolled = pltpu.roll(theirs, fields, 1)
    rows = jnp.where(lane < fields, mine[0:1], rolled[0:1])
    slots = jnp.where(lane < fields, mine[1:2], rolled[1:2] - half)
    place = lax.broadcasted_iota(jnp.int32, (width, width), 0).astype(jnp.float32)
    part = lax.broadcasted_iota(jnp.int32, (width, width), 1) // fields
    sign = jnp.where(core == 0, 0.5, -0.5)
    columns = jnp.zeros((fields, width), jnp.float32)
    for k, (block, factor) in enumerate(zip((got_ref[half + 1], sent_ref[half + 1]), (sign, -sign))):
        pick = jnp.where((place == rows) & (part == k), factor, 0.0).astype(jnp.bfloat16)
        columns = columns + jnp.dot(block, pick, preferred_element_type=jnp.float32)
    for t in range(half):
        select[t * fields : (t + 1) * fields] = jnp.where(slots == t, columns, 0.0).astype(jnp.bfloat16)
    edges[...] = jnp.zeros_like(edges)
    edges[0:fields] = sent_ref[half]
    edges[fields : 2 * fields] = got_ref[half]
    for k in range(chips):
        span = slice(k * count, (k + 1) * count)
        border = jnp.dot(
            select[k * count * fields : (k + 1) * count * fields], edges[...], preferred_element_type=jnp.float32
        )
        total = keep_ref[span] + got_ref[span].astype(jnp.float32) + border.reshape(count, fields, width)
        if k == 0:
            own_ref[...] = total
        out_ref[along ^ k, 0:count] = total.astype(jnp.bfloat16)
    first = core == 0
    outer = sent_ref[half + 4] + got_ref[half + 4]
    vectors = jnp.where(
        lax.broadcasted_iota(jnp.int32, mine.shape, 0) < 8,
        jnp.where(first, mine, theirs),
        pltpu.roll(jnp.where(first, theirs, mine), 8, 0),
    ).astype(jnp.bfloat16) + outer
    sides = [jnp.where(first == (k == 0), sent_ref[half + 3], got_ref[half + 3]) for k in range(2)]
    for k in range(chips):
        for i, block in enumerate((*sides, vectors)):
            out_ref[k, count + i] = block


def total_kernel(own_ref, got_ref, here_ref, next_ref, select, edges):
    sub = lax.axis_index("sub")
    along = sub // 2
    count, fields, width = own_ref.shape
    chips, rows = got_ref.shape[0], 8
    sets = width // fields
    lane = lax.broadcasted_iota(jnp.int32, (1, width), 1)
    place = lax.broadcasted_iota(jnp.int32, (width, width), 0).astype(jnp.float32)
    total = own_ref[...]
    for k in range(1, chips):
        total = total + got_ref[along ^ k, 0:count].astype(jnp.float32)
    for group in range(2 * chips // sets):
        columns = jnp.zeros((fields, width), jnp.float32)
        targets = jnp.full((1, width), -1.0, jnp.float32)
        for i in range(sets):
            chip, core = divmod(group * sets + i, 2)
            edges[group, i * fields : (i + 1) * fields] = got_ref[chip, count + core]
            vectors = got_ref[chip, count + 2].astype(jnp.float32)
            if i:
                vectors = pltpu.roll(vectors, i * fields, 1)
            inside = (lane >= i * fields) & (lane < (i + 1) * fields)
            targets = jnp.where(inside, vectors[8 * core + 2 : 8 * core + 3], targets)
            beside = chip + 2 * core - 1
            if 0 <= beside < chips:
                source = vectors[8 * core : 8 * core + 1] + (OUTER if core else OUTER + rows)
                pick = jnp.where((place == source) & inside, 0.5 if core else -0.5, 0.0).astype(jnp.bfloat16)
                columns = columns + jnp.dot(got_ref[beside, count + 2], pick, preferred_element_type=jnp.float32)
        targets = targets - (sub * count).astype(jnp.float32)
        for t in range(count):
            select[t * fields : (t + 1) * fields] = jnp.where(targets == t, columns, 0.0).astype(jnp.bfloat16)
        border = jnp.dot(select[...], edges[group], preferred_element_type=jnp.float32)
        total = total + border.reshape(count, fields, width)
    here_ref[...] = total[:OB_DEV]
    next_ref[...] = total[OB_DEV:].astype(jnp.bfloat16)


def final_kernel(here_ref, got_ref, out_ref):
    for q in range(OB_DEV):
        out_ref[:, q * LANES : (q + 1) * LANES] = here_ref[q] + got_ref[q].astype(jnp.float32)


def shards(atmos_flux, weight_tiles, source_row, target_code, live_count):
    fields, rows, width = atmos_flux.shape
    capacity = weight_tiles.shape[2]
    subs, bands = lax.axis_size("sub"), lax.axis_size("band")
    blocks = 2 * OB_DEV
    half = subs // 2 * blocks
    params = pltpu.CompilerParams(vmem_limit_bytes=24 * 2**20)
    far = lax.ppermute(atmos_flux, "band", swap_pairs(bands, 1))
    pairs = swap_pairs(bands, 0)
    first = lax.ppermute(atmos_flux, "band", [p for p in pairs if min(p) % PLANE == 0])
    near = lax.ppermute(atmos_flux, "band", [p for p in pairs if min(p) % PLANE != 0])
    sums = jax.ShapeDtypeStruct((2 * half + 1, fields, width), jnp.float32)
    indices = (hbm(source_row), hbm(target_code))
    index_scratch = [pltpu.SMEM(a.shape, a.dtype) for a in indices]
    tiles = hbm(weight_tiles[0, 0])
    meta = jax.ShapeDtypeStruct((5, fields, width), jnp.bfloat16)
    acc, held, meta = pl.pallas_call(
        inner_kernel,
        out_shape=(sums, jax.ShapeDtypeStruct(tiles.shape, tiles.dtype), meta),
        in_specs=[HBM, HBM, SMEM, HBM, HBM],
        out_specs=(VMEM, VMEM, VMEM),
        scratch_shapes=index_scratch + [pltpu.VMEM(a.shape, a.dtype) for a in indices] + [
            pltpu.VMEM((fields, rows, width), atmos_flux.dtype),
            pltpu.VMEM((2, fields * rows, width), jnp.float32),
            pltpu.VMEM((rows, fields, 3 * width), jnp.bfloat16),
            pltpu.VMEM((2, capacity, width), jnp.float32),
            pltpu.SemaphoreType.DMA((4,)),
            pltpu.SemaphoreType.DMA,
            pltpu.SemaphoreType.DMA((capacity // GROUP,)),
        ],
        compiler_params=params,
        cost_estimate=pl.CostEstimate(flops=100_000_000, bytes_accessed=6_000_000, transcendentals=0),
        name="inner",
    )(*indices, live_count, hbm(atmos_flux), tiles)
    payload = jax.ShapeDtypeStruct((half + 5, fields, width), jnp.bfloat16)
    acc, send = pl.pallas_call(
        border_kernel,
        out_shape=(sums, payload),
        in_specs=[HBM, HBM, SMEM] + [VMEM] * 6,
        out_specs=(VMEM, VMEM),
        scratch_shapes=index_scratch + [
            pltpu.VMEM((2, fields * rows, width), jnp.float32),
            pltpu.VMEM((rows, fields, width), jnp.bfloat16),
            pltpu.SemaphoreType.DMA((2,)),
        ],
        input_output_aliases={8: 0},
        compiler_params=params,
        cost_estimate=pl.CostEstimate(flops=30_000_000, bytes_accessed=4_000_000, transcendentals=0),
        name="border",
    )(*indices, live_count, far, first, near, held, meta, acc)
    got = lax.ppermute(send, "sub", xor_pairs(subs, 1))
    own, outs = pl.pallas_call(
        pair_sum_kernel,
        out_shape=(
            jax.ShapeDtypeStruct((blocks, fields, width), jnp.float32),
            jax.ShapeDtypeStruct((subs // 2, blocks + 3, fields, width), jnp.bfloat16),
        ),
        in_specs=[VMEM] * 3,
        out_specs=(VMEM, VMEM),
        scratch_shapes=[
            pltpu.VMEM((half * fields, width), jnp.bfloat16),
            pltpu.VMEM((width, width), jnp.bfloat16),
        ],
        compiler_params=params,
        name="pair_sum",
    )(acc, send, got)
    groups = [list(range(core, subs, 2)) for core in range(2)]
    arrived = lax.all_to_all(outs, "sub", split_axis=0, concat_axis=0, axis_index_groups=groups, tiled=True)
    here, ahead = pl.pallas_call(
        total_kernel,
        out_shape=(
            jax.ShapeDtypeStruct((OB_DEV, fields, width), jnp.float32),
            jax.ShapeDtypeStruct((OB_DEV, fields, width), jnp.bfloat16),
        ),
        in_specs=[VMEM] * 2,
        out_specs=(VMEM, VMEM),
        scratch_shapes=[
            pltpu.VMEM((blocks * fields, width), jnp.bfloat16),
            pltpu.VMEM((subs * fields // width, width, width), jnp.bfloat16),
        ],
        compiler_params=params,
        name="total",
    )(own, arrived)
    behind = lax.ppermute(ahead, "band", [(i, (i + 1) % bands) for i in range(bands)])
    return pl.pallas_call(
        final_kernel,
        out_shape=jax.ShapeDtypeStruct((fields, OB_DEV * width), jnp.float32),
        in_specs=[VMEM] * 2,
        out_specs=VMEM,
        compiler_params=params,
        name="final",
    )(here, behind)


def solution(mesh):
    return jax.shard_map(
        shards,
        mesh=mesh,
        in_specs=(
            P(None, "band", "sub"),
            P("band", "sub", None, None, None),
            P("band", "sub", None),
            P("band", "sub", None),
            P("band", "sub"),
        ),
        out_specs=P(None, ("band", "sub")),
        check_vma=False,
    )
```

time: 57.9 us -> 54.2 us (0.936); the launches traced: 57.1 us -> 54 us
  starting transfers between devices: 32.2 us -> 24.1 us
  waiting for transfers between devices: 6.22 us -> 8.28 us
  blocking collectives: 13.7 us -> 15.7 us
  Pallas kernels: 4.19 us -> 5.22 us
    ppermute x1, starting transfers between devices: 18.9 us -> 15.8 us  [shards(): far = lax.ppermute(atmos_flux, 'band', swap_pairs(bands, 1))]
    ppermute x3 -> x2, starting transfers between devices: 7.43 us -> 4.48 us  [the longest x1 3.81 us: shards(): lax.ppermute(atmos_flux, 'band', [p for p in pairs if min(p) % PLANE == 0])]
    ppermute x1, starting transfers between devices: 3.92 us -> 1.92 us  [shards(): lax.ppermute(ahead, 'band', [(i, (i + 1) % bands) for i in range(bands)])]
    ppermute x1, waiting for transfers between devices: 4.34 us -> 6.34 us  [shards(): lax.ppermute(ahead, 'band', [(i, (i + 1) % bands) for i in range(bands)])]
    all_to_all x1, blocking collectives: 13.7 us -> 15.7 us  [shards(): lax.all_to_all(outs, 'sub', split_axis=0, concat_axis=0, axis_index_group...]
  transfers between devices with their start and end apart: 6 -> 5, of which waited for: 2 -> 2; matrix products, arithmetic and copies ran while one was open for 0% -> 0% of each run, Pallas kernels for 4% -> 4%
where the time goes in v4:
time: 54.2 us; the launch traced here: 54 us
  starting transfers between devices  24.1 us (44%)
  blocking collectives  15.7 us (29%)
  waiting for transfers between devices  8.28 us (15%)
  Pallas kernels  5.22 us (10%)
  between operations  0.74 us (1%)
    ppermute x1, starting transfers between devices, shards(): far = lax.ppermute(atmos_flux, 'band', swap_pairs(bands, 1))  15.8 us
    all_to_all x1, blocking collectives, shards(): lax.all_to_all(outs, 'sub', split_axis=0, concat_axis=0, axis_index_group...  15.7 us
    ppermute x1, waiting for transfers between devices, shards(): lax.ppermute(ahead, 'band', [(i, (i + 1) % bands) for i in range(bands)])  6.34 us
    ppermute x1, starting transfers between devices, shards(): lax.ppermute(atmos_flux, 'band', [p for p in pairs if min(p) % PLANE == 0])  3.81 us
    pallas_call x1, Pallas kernels, shards(): pl.pallas_call(inner_kernel, out_shape=(sums, jax.ShapeDtypeStruct(tiles....  2.3 us
    ppermute x1, waiting for transfers between devices, shards(): got = lax.ppermute(send, 'sub', xor_pairs(subs, 1))  1.93 us
    ppermute x1, starting transfers between devices, shards(): got = lax.ppermute(send, 'sub', xor_pairs(subs, 1))  1.92 us
    ppermute x1, starting transfers between devices, shards(): lax.ppermute(ahead, 'band', [(i, (i + 1) % bands) for i in range(bands)])  1.92 us
  transfers between devices with their start and end apart: 5, of which 2 were waited for; matrix products, arithmetic and copies ran while one was open for 0% of the time, Pallas kernels for 4%

profile of v4, /device:TPU:6, one launch (start us, length us, event | category | flops | bytes accessed | tf_op | source)
XLA Modules:
  0.0 54.0 jit_solution(2589238050053040001)
XLA Ops:
  0.0 3.8 %collective-permute-start.1 = (bf16[32,8,128]{2,1,0:T(8,128)(2,1)}, bf16[32,8,128]{2,1,0:T(8,128)(2,1)S(1)}, u32[]{:S(2)}, u32[]{:S(2)}) collective-permute-start(bf16[32,8,128]{2,1,0:T(8,128)(2,1)} %x_hbm.1), channel_id=1, source_target_pairs={{0,8},{8,0},{256,264},{264,256},{512,520},{520,512},{768,776},{776... | collective-permute-start | bytes 196616 | tf_op jit(solution)/shard_map/ppermute | solution.py:276
  3.8 15.8 %collective-permute-start = (bf16[32,8,128]{2,1,0:T(8,128)(2,1)}, bf16[32,8,128]{2,1,0:T(8,128)(2,1)S(1)}, u32[]{:S(2)}, u32[]{:S(2)}) collective-permute-start(bf16[32,8,128]{2,1,0:T(8,128)(2,1)} %x_hbm.1), channel_id=1, source_target_pairs={{8,16},{16,8},{24,32},{32,24},{40,48},{48,40},{56,64},{64,56},{72,... | collective-permute-start | bytes 196616 | tf_op jit(solution)/shard_map/ppermute | solution.py:274
  19.6 0.7 %collective-permute-start.2 = (bf16[32,8,128]{2,1,0:T(8,128)(2,1)}, bf16[32,8,128]{2,1,0:T(8,128)(2,1)S(1)}, u32[]{:S(2)}, u32[]{:S(2)}) collective-permute-start(bf16[32,8,128]{2,1,0:T(8,128)(2,1)} %x_hbm.1), channel_id=1, source_target_pairs={{16,24},{24,16},{32,40},{40,32},{48,56},{56,48},{64,72},{72,64},{8... | collective-permute-start | bytes 196616 | tf_op jit(solution)/shard_map/ppermute | solution.py:277
  20.9 2.3 %inner.1 = (f32[129,32,128]{2,1,0:T(8,128)S(1)}, bf16[32,384,128]{2,1,0:T(8,128)(2,1)S(1)}, bf16[5,32,128]{2,1,0:T(8,128)(2,1)S(1)}) custom-call(s32[1,1,32]{2,1,0:T(1,128)} %row_hbm.3, s32[1,1,32]{2,1,0:T(1,128)} %code_hbm.3, s32[1,1]{1,0:T(1,128)S(6)} %copy.8.live_ref, bf16[32,8,128]{2,1,0:T(8,128)(2,1)} %x_hbm.1, bf16[32,384,128]{2,1,0:T(8,128)(2,1)} %bitcast.1), custom_call_target="tpu_custom_call" | custom-call | flops 100000000 | bytes 6000000 | tf_op jit(solution)/shard_map/inner/pallas_call | solution.py:283
  23.2 0.0 collective-permute-done.1.first_ref
  23.2 0.0 collective-permute-done.far_ref
  23.3 0.0 collective-permute-done.2.near_ref
  23.3 1.1 %border.1 = (f32[129,32,128]{2,1,0:T(8,128)S(1)}, bf16[69,32,128]{2,1,0:T(8,128)(2,1)S(1)}) custom-call(s32[1,1,32]{2,1,0:T(1,128)} %row_hbm.3, s32[1,1,32]{2,1,0:T(1,128)} %code_hbm.3, s32[1,1]{1,0:T(1,128)S(6)} %copy.8.live_ref, bf16[32,8,128]{2,1,0:T(8,128)(2,1)S(1)} %collective-permute-done.far_ref, ...), custom_call_target="tpu_custom_call", output_to_operand_aliasing={{0}: (8, {})} | custom-call | flops 30000000 | bytes 4000000 | tf_op jit(solution)/shard_map/border/pallas_call | solution.py:302
  24.4 1.9 %collective-permute-start.3 = (bf16[69,32,128]{2,1,0:T(8,128)(2,1)S(1)}, bf16[69,32,128]{2,1,0:T(8,128)(2,1)S(1)}, u32[]{:S(2)}, u32[]{:S(2)}) collective-permute-start(bf16[69,32,128]{2,1,0:T(8,128)(2,1)S(1)} %get-tuple-element.18.sent_ref), channel_id=1, source_target_pairs={{0,1},{1,0},{2,3},{3,2},{4,5},{5,4},{6,7},{7,6},{8,9},{9,8},{10,11... | collective-permute-start | bytes 1695752 | tf_op jit(solution)/shard_map/ppermute | solution.py:317
  26.3 1.9 %collective-permute-done.3.got_ref = bf16[69,32,128]{2,1,0:T(8,128)(2,1)S(1)} collective-permute-done((bf16[69,32,128]{2,1,0:T(8,128)(2,1)S(1)}, bf16[69,32,128]{2,1,0:T(8,128)(2,1)S(1)}, u32[]{:S(2)}, u32[]{:S(2)}) %collective-permute-start.3) | collective-permute-done | bytes 565280 | tf_op jit(solution)/shard_map/ppermute | solution.py:317
  28.3 0.5 pair_sum.1
  28.8 15.7 %all_to_all.5.got_ref = bf16[4,19,32,128]{3,2,1,0:T(8,128)(2,1)S(1)} all-to-all(bf16[4,19,32,128]{3,2,1,0:T(8,128)(2,1)S(1)} %get-tuple-element.20), channel_id=1, replica_groups={{0,2,4,6},{1,3,5,7},{8,10,12,14},{9,11,13,15},{16,18,20,22},{17,19,21,2..., dimensions={0} | all-to-all | bytes 1245184 | tf_op jit(solution)/shard_map/all_to_all | solution.py:334
  44.4 0.6 %total.1 = (f32[8,32,128]{2,1,0:T(8,128)S(1)}, bf16[8,32,128]{2,1,0:T(8,128)(2,1)S(1)}) custom-call(f32[16,32,128]{2,1,0:T(8,128)S(1)} %get-tuple-element.19.own_ref, bf16[4,19,32,128]{3,2,1,0:T(8,128)(2,1)S(1)} %all_to_all.5.got_ref), custom_call_target="tpu_custom_call" | custom-call | tf_op jit(solution)/shard_map/total/pallas_call | solution.py:335
  45.1 1.9 %collective-permute-start.4 = (bf16[8,32,128]{2,1,0:T(8,128)(2,1)S(1)}, bf16[8,32,128]{2,1,0:T(8,128)(2,1)S(1)}, u32[]{:S(2)}, u32[]{:S(2)}) collective-permute-start(bf16[8,32,128]{2,1,0:T(8,128)(2,1)S(1)} %get-tuple-element.22), channel_id=1, source_target_pairs={{0,8},{8,16},{16,24},{24,32},{32,40},{40,48},{48,56},{56,64},{64,7... | collective-permute-start | bytes 196616 | tf_op jit(solution)/shard_map/ppermute | solution.py:350
  47.0 6.3 %collective-permute-done.4.got_ref = bf16[8,32,128]{2,1,0:T(8,128)(2,1)S(1)} collective-permute-done((bf16[8,32,128]{2,1,0:T(8,128)(2,1)S(1)}, bf16[8,32,128]{2,1,0:T(8,128)(2,1)S(1)}, u32[]{:S(2)}, u32[]{:S(2)}) %collective-permute-start.4) | collective-permute-done | bytes 65568 | tf_op jit(solution)/shard_map/ppermute | solution.py:350
  53.3 0.7 %final.1 = f32[32,1024]{1,0:T(8,128)} custom-call(f32[8,32,128]{2,1,0:T(8,128)S(1)} %get-tuple-element.21.here_ref, bf16[8,32,128]{2,1,0:T(8,128)(2,1)S(1)} %collective-permute-done.4.got_ref), custom_call_target="tpu_custom_call" | custom-call | tf_op jit(solution)/shard_map/final/pallas_call | solution.py:351
Async XLA Ops:
  0.0 23.2 %collective-permute-start.1 = (bf16[32,8,128]{2,1,0:T(8,128)(2,1)}, bf16[32,8,128]{2,1,0:T(8,128)(2,1)S(1)}, u32[]{:S(2)}, u32[]{:S(2)}) collective-permute-start(bf16[32,8,128]{2,1,0:T(8,128)(2,1)} %x_hbm.1), channel_id=1, source_target_pairs={{0,8},{8,0},{256,264},{264,256},{512,520},{520,512},{768,776},{776... | collective-permute-start | bytes 196616 | tf_op jit(solution)/shard_map/ppermute | solution.py:276
  3.8 19.4 %collective-permute-start = (bf16[32,8,128]{2,1,0:T(8,128)(2,1)}, bf16[32,8,128]{2,1,0:T(8,128)(2,1)S(1)}, u32[]{:S(2)}, u32[]{:S(2)}) collective-permute-start(bf16[32,8,128]{2,1,0:T(8,128)(2,1)} %x_hbm.1), channel_id=1, source_target_pairs={{8,16},{16,8},{24,32},{32,24},{40,48},{48,40},{56,64},{64,56},{72,... | collective-permute-start | bytes 196616 | tf_op jit(solution)/shard_map/ppermute | solution.py:274
  19.6 3.6 %collective-permute-start.2 = (bf16[32,8,128]{2,1,0:T(8,128)(2,1)}, bf16[32,8,128]{2,1,0:T(8,128)(2,1)S(1)}, u32[]{:S(2)}, u32[]{:S(2)}) collective-permute-start(bf16[32,8,128]{2,1,0:T(8,128)(2,1)} %x_hbm.1), channel_id=1, source_target_pairs={{16,24},{24,16},{32,40},{40,32},{48,56},{56,48},{64,72},{72,64},{8... | collective-permute-start | bytes 196616 | tf_op jit(solution)/shard_map/ppermute | solution.py:277
  24.4 3.9 %collective-permute-start.3 = (bf16[69,32,128]{2,1,0:T(8,128)(2,1)S(1)}, bf16[69,32,128]{2,1,0:T(8,128)(2,1)S(1)}, u32[]{:S(2)}, u32[]{:S(2)}) collective-permute-start(bf16[69,32,128]{2,1,0:T(8,128)(2,1)S(1)} %get-tuple-element.18.sent_ref), channel_id=1, source_target_pairs={{0,1},{1,0},{2,3},{3,2},{4,5},{5,4},{6,7},{7,6},{8,9},{9,8},{10,11... | collective-permute-start | bytes 1695752 | tf_op jit(solution)/shard_map/ppermute | solution.py:317
  45.1 8.3 %collective-permute-start.4 = (bf16[8,32,128]{2,1,0:T(8,128)(2,1)S(1)}, bf16[8,32,128]{2,1,0:T(8,128)(2,1)S(1)}, u32[]{:S(2)}, u32[]{:S(2)}) collective-permute-start(bf16[8,32,128]{2,1,0:T(8,128)(2,1)S(1)} %get-tuple-element.22), channel_id=1, source_target_pairs={{0,8},{8,16},{16,24},{24,32},{32,40},{40,48},{48,56},{56,64},{64,7... | collective-permute-start | bytes 196616 | tf_op jit(solution)/shard_map/ppermute | solution.py:350

commit v5 on v4

--- a/solution.py
+++ b/solution.py
@@ -89,8 +89,8 @@
     lane = lax.broadcasted_iota(jnp.int32, (flat, width), 1)
     later = pltpu.roll(jnp.where(lane == 0, 0.0, x), width - 1, 1)
     earlier = pltpu.roll(jnp.where(lane == width - 1, 0.0, x), 1, 1)
-    xf[0] = x
-    xf[1] = 0.5 * (later - earlier)
+    xf[0, 0:flat] = x
+    xf[1, 0:flat] = 0.5 * (later - earlier)
 
     def row(which, r):
         return xf[which, pl.ds(r, fields, stride=rows), :]
@@ -152,8 +152,8 @@
         ref[...].astype(jnp.float32).reshape(flat, width) for ref in (near_ref, first_ref, far_ref)
     )
     near = near + first
-    xf[0] = -0.5 * jnp.where(odd_band, near, far)
-    xf[1] = 0.5 * jnp.where(odd_band, far, near)
+    xf[0, 0:flat] = -0.5 * jnp.where(odd_band, near, far)
+    xf[1, 0:flat] = 0.5 * jnp.where(odd_band, far, near)
     ends[...] = jnp.zeros_like(ends)
     ends[0] = xf[0, pl.ds(rows - 1, fields, stride=rows), :].astype(jnp.bfloat16)
     ends[rows - 1] = xf[1, pl.ds(0, fields, stride=rows), :].astype(jnp.bfloat16)
@@ -287,7 +287,7 @@
         out_specs=(VMEM, VMEM, VMEM),
         scratch_shapes=index_scratch + [pltpu.VMEM(a.shape, a.dtype) for a in indices] + [
             pltpu.VMEM((fields, rows, width), atmos_flux.dtype),
-            pltpu.VMEM((2, fields * rows, width), jnp.float32),
+            pltpu.VMEM((2, fields * rows + rows, width), jnp.float32),
             pltpu.VMEM((rows, fields, 3 * width), jnp.bfloat16),
             pltpu.VMEM((2, capacity, width), jnp.float32),
             pltpu.SemaphoreType.DMA((4,)),
@@ -305,7 +305,7 @@
         in_specs=[HBM, HBM, SMEM] + [VMEM] * 6,
         out_specs=(VMEM, VMEM),
         scratch_shapes=index_scratch + [
-            pltpu.VMEM((2, fields * rows, width), jnp.float32),
+            pltpu.VMEM((2, fields * rows + rows, width), jnp.float32),
             pltpu.VMEM((rows, fields, width), jnp.bfloat16),
             pltpu.SemaphoreType.DMA((2,)),
         ],

time: 54.2 us -> 54.2 us (level); the launches traced: 54 us -> 53.4 us
  blocking collectives: 15.7 us -> 15.1 us
    all_to_all x1, blocking collectives: 15.7 us -> 15.1 us  [shards(): lax.all_to_all(outs, 'sub', split_axis=0, concat_axis=0, axis_index_group...]
where the time goes in v5:
time: 54.2 us; the launch traced here: 53.4 us
  starting transfers between devices  24.1 us (44%)
  blocking collectives  15.1 us (28%)
  waiting for transfers between devices  8.28 us (15%)
  Pallas kernels  5.22 us (10%)
  between operations  0.74 us (1%)
    ppermute x1, starting transfers between devices, shards(): far = lax.ppermute(atmos_flux, 'band', swap_pairs(bands, 1))  15.8 us
    all_to_all x1, blocking collectives, shards(): lax.all_to_all(outs, 'sub', split_axis=0, concat_axis=0, axis_index_group...  15.1 us
    ppermute x1, waiting for transfers between devices, shards(): lax.ppermute(ahead, 'band', [(i, (i + 1) % bands) for i in range(bands)])  6.34 us
    ppermute x1, starting transfers between devices, shards(): lax.ppermute(atmos_flux, 'band', [p for p in pairs if min(p) % PLANE == 0])  3.81 us
    pallas_call x1, Pallas kernels, shards(): pl.pallas_call(inner_kernel, out_shape=(sums, jax.ShapeDtypeStruct(tiles....  2.3 us
    ppermute x1, waiting for transfers between devices, shards(): got = lax.ppermute(send, 'sub', xor_pairs(subs, 1))  1.93 us
    ppermute x1, starting transfers between devices, shards(): lax.ppermute(ahead, 'band', [(i, (i + 1) % bands) for i in range(bands)])  1.92 us
    ppermute x1, starting transfers between devices, shards(): got = lax.ppermute(send, 'sub', xor_pairs(subs, 1))  1.92 us
  transfers between devices with their start and end apart: 5, of which 2 were waited for; matrix products, arithmetic and copies ran while one was open for 0% of the time, Pallas kernels for 4%

profile of v5, /device:TPU:6, one launch (start us, length us, event | category | flops | bytes accessed | tf_op | source)
XLA Modules:
  0.0 53.4 jit_solution(16329763259428930912)
XLA Ops:
  0.0 3.8 %collective-permute-start.1 = (bf16[32,8,128]{2,1,0:T(8,128)(2,1)}, bf16[32,8,128]{2,1,0:T(8,128)(2,1)S(1)}, u32[]{:S(2)}, u32[]{:S(2)}) collective-permute-start(bf16[32,8,128]{2,1,0:T(8,128)(2,1)} %x_hbm.1), channel_id=1, source_target_pairs={{0,8},{8,0},{256,264},{264,256},{512,520},{520,512},{768,776},{776... | collective-permute-start | bytes 196616 | tf_op jit(solution)/shard_map/ppermute | solution.py:276
  3.8 15.8 %collective-permute-start = (bf16[32,8,128]{2,1,0:T(8,128)(2,1)}, bf16[32,8,128]{2,1,0:T(8,128)(2,1)S(1)}, u32[]{:S(2)}, u32[]{:S(2)}) collective-permute-start(bf16[32,8,128]{2,1,0:T(8,128)(2,1)} %x_hbm.1), channel_id=1, source_target_pairs={{8,16},{16,8},{24,32},{32,24},{40,48},{48,40},{56,64},{64,56},{72,... | collective-permute-start | bytes 196616 | tf_op jit(solution)/shard_map/ppermute | solution.py:274
  19.6 0.7 %collective-permute-start.2 = (bf16[32,8,128]{2,1,0:T(8,128)(2,1)}, bf16[32,8,128]{2,1,0:T(8,128)(2,1)S(1)}, u32[]{:S(2)}, u32[]{:S(2)}) collective-permute-start(bf16[32,8,128]{2,1,0:T(8,128)(2,1)} %x_hbm.1), channel_id=1, source_target_pairs={{16,24},{24,16},{32,40},{40,32},{48,56},{56,48},{64,72},{72,64},{8... | collective-permute-start | bytes 196616 | tf_op jit(solution)/shard_map/ppermute | solution.py:277
  20.9 2.3 %inner.1 = (f32[129,32,128]{2,1,0:T(8,128)S(1)}, bf16[32,384,128]{2,1,0:T(8,128)(2,1)S(1)}, bf16[5,32,128]{2,1,0:T(8,128)(2,1)S(1)}) custom-call(s32[1,1,32]{2,1,0:T(1,128)} %row_hbm.3, s32[1,1,32]{2,1,0:T(1,128)} %code_hbm.3, s32[1,1]{1,0:T(1,128)S(6)} %copy.8.live_ref, bf16[32,8,128]{2,1,0:T(8,128)(2,1)} %x_hbm.1, bf16[32,384,128]{2,1,0:T(8,128)(2,1)} %bitcast.1), custom_call_target="tpu_custom_call" | custom-call | flops 100000000 | bytes 6000000 | tf_op jit(solution)/shard_map/inner/pallas_call | solution.py:283
  23.2 0.0 collective-permute-done.1.first_ref
  23.2 0.0 collective-permute-done.far_ref
  23.3 0.0 collective-permute-done.2.near_ref
  23.3 1.1 %border.1 = (f32[129,32,128]{2,1,0:T(8,128)S(1)}, bf16[69,32,128]{2,1,0:T(8,128)(2,1)S(1)}) custom-call(s32[1,1,32]{2,1,0:T(1,128)} %row_hbm.3, s32[1,1,32]{2,1,0:T(1,128)} %code_hbm.3, s32[1,1]{1,0:T(1,128)S(6)} %copy.8.live_ref, bf16[32,8,128]{2,1,0:T(8,128)(2,1)S(1)} %collective-permute-done.far_ref, ...), custom_call_target="tpu_custom_call", output_to_operand_aliasing={{0}: (8, {})} | custom-call | flops 30000000 | bytes 4000000 | tf_op jit(solution)/shard_map/border/pallas_call | solution.py:302
  24.4 1.9 %collective-permute-start.3 = (bf16[69,32,128]{2,1,0:T(8,128)(2,1)S(1)}, bf16[69,32,128]{2,1,0:T(8,128)(2,1)S(1)}, u32[]{:S(2)}, u32[]{:S(2)}) collective-permute-start(bf16[69,32,128]{2,1,0:T(8,128)(2,1)S(1)} %get-tuple-element.18.sent_ref), channel_id=1, source_target_pairs={{0,1},{1,0},{2,3},{3,2},{4,5},{5,4},{6,7},{7,6},{8,9},{9,8},{10,11... | collective-permute-start | bytes 1695752 | tf_op jit(solution)/shard_map/ppermute | solution.py:317
  26.3 1.9 %collective-permute-done.3.got_ref = bf16[69,32,128]{2,1,0:T(8,128)(2,1)S(1)} collective-permute-done((bf16[69,32,128]{2,1,0:T(8,128)(2,1)S(1)}, bf16[69,32,128]{2,1,0:T(8,128)(2,1)S(1)}, u32[]{:S(2)}, u32[]{:S(2)}) %collective-permute-start.3) | collective-permute-done | bytes 565280 | tf_op jit(solution)/shard_map/ppermute | solution.py:317
  28.3 0.5 pair_sum.1
  28.8 15.1 %all_to_all.5.got_ref = bf16[4,19,32,128]{3,2,1,0:T(8,128)(2,1)S(1)} all-to-all(bf16[4,19,32,128]{3,2,1,0:T(8,128)(2,1)S(1)} %get-tuple-element.20), channel_id=1, replica_groups={{0,2,4,6},{1,3,5,7},{8,10,12,14},{9,11,13,15},{16,18,20,22},{17,19,21,2..., dimensions={0} | all-to-all | bytes 1245184 | tf_op jit(solution)/shard_map/all_to_all | solution.py:334
  43.9 0.6 %total.1 = (f32[8,32,128]{2,1,0:T(8,128)S(1)}, bf16[8,32,128]{2,1,0:T(8,128)(2,1)S(1)}) custom-call(f32[16,32,128]{2,1,0:T(8,128)S(1)} %get-tuple-element.19.own_ref, bf16[4,19,32,128]{3,2,1,0:T(8,128)(2,1)S(1)} %all_to_all.5.got_ref), custom_call_target="tpu_custom_call" | custom-call | tf_op jit(solution)/shard_map/total/pallas_call | solution.py:335
  44.5 1.9 %collective-permute-start.4 = (bf16[8,32,128]{2,1,0:T(8,128)(2,1)S(1)}, bf16[8,32,128]{2,1,0:T(8,128)(2,1)S(1)}, u32[]{:S(2)}, u32[]{:S(2)}) collective-permute-start(bf16[8,32,128]{2,1,0:T(8,128)(2,1)S(1)} %get-tuple-element.22), channel_id=1, source_target_pairs={{0,8},{8,16},{16,24},{24,32},{32,40},{40,48},{48,56},{56,64},{64,7... | collective-permute-start | bytes 196616 | tf_op jit(solution)/shard_map/ppermute | solution.py:350
  46.4 6.3 %collective-permute-done.4.got_ref = bf16[8,32,128]{2,1,0:T(8,128)(2,1)S(1)} collective-permute-done((bf16[8,32,128]{2,1,0:T(8,128)(2,1)S(1)}, bf16[8,32,128]{2,1,0:T(8,128)(2,1)S(1)}, u32[]{:S(2)}, u32[]{:S(2)}) %collective-permute-start.4) | collective-permute-done | bytes 65568 | tf_op jit(solution)/shard_map/ppermute | solution.py:350
  52.8 0.7 %final.1 = f32[32,1024]{1,0:T(8,128)} custom-call(f32[8,32,128]{2,1,0:T(8,128)S(1)} %get-tuple-element.21.here_ref, bf16[8,32,128]{2,1,0:T(8,128)(2,1)S(1)} %collective-permute-done.4.got_ref), custom_call_target="tpu_custom_call" | custom-call | tf_op jit(solution)/shard_map/final/pallas_call | solution.py:351
Async XLA Ops:
  0.0 23.2 %collective-permute-start.1 = (bf16[32,8,128]{2,1,0:T(8,128)(2,1)}, bf16[32,8,128]{2,1,0:T(8,128)(2,1)S(1)}, u32[]{:S(2)}, u32[]{:S(2)}) collective-permute-start(bf16[32,8,128]{2,1,0:T(8,128)(2,1)} %x_hbm.1), channel_id=1, source_target_pairs={{0,8},{8,0},{256,264},{264,256},{512,520},{520,512},{768,776},{776... | collective-permute-start | bytes 196616 | tf_op jit(solution)/shard_map/ppermute | solution.py:276
  3.8 19.4 %collective-permute-start = (bf16[32,8,128]{2,1,0:T(8,128)(2,1)}, bf16[32,8,128]{2,1,0:T(8,128)(2,1)S(1)}, u32[]{:S(2)}, u32[]{:S(2)}) collective-permute-start(bf16[32,8,128]{2,1,0:T(8,128)(2,1)} %x_hbm.1), channel_id=1, source_target_pairs={{8,16},{16,8},{24,32},{32,24},{40,48},{48,40},{56,64},{64,56},{72,... | collective-permute-start | bytes 196616 | tf_op jit(solution)/shard_map/ppermute | solution.py:274
  19.6 3.6 %collective-permute-start.2 = (bf16[32,8,128]{2,1,0:T(8,128)(2,1)}, bf16[32,8,128]{2,1,0:T(8,128)(2,1)S(1)}, u32[]{:S(2)}, u32[]{:S(2)}) collective-permute-start(bf16[32,8,128]{2,1,0:T(8,128)(2,1)} %x_hbm.1), channel_id=1, source_target_pairs={{16,24},{24,16},{32,40},{40,32},{48,56},{56,48},{64,72},{72,64},{8... | collective-permute-start | bytes 196616 | tf_op jit(solution)/shard_map/ppermute | solution.py:277
  24.4 3.9 %collective-permute-start.3 = (bf16[69,32,128]{2,1,0:T(8,128)(2,1)S(1)}, bf16[69,32,128]{2,1,0:T(8,128)(2,1)S(1)}, u32[]{:S(2)}, u32[]{:S(2)}) collective-permute-start(bf16[69,32,128]{2,1,0:T(8,128)(2,1)S(1)} %get-tuple-element.18.sent_ref), channel_id=1, source_target_pairs={{0,1},{1,0},{2,3},{3,2},{4,5},{5,4},{6,7},{7,6},{8,9},{9,8},{10,11... | collective-permute-start | bytes 1695752 | tf_op jit(solution)/shard_map/ppermute | solution.py:317
  44.5 8.3 %collective-permute-start.4 = (bf16[8,32,128]{2,1,0:T(8,128)(2,1)S(1)}, bf16[8,32,128]{2,1,0:T(8,128)(2,1)S(1)}, u32[]{:S(2)}, u32[]{:S(2)}) collective-permute-start(bf16[8,32,128]{2,1,0:T(8,128)(2,1)S(1)} %get-tuple-element.22), channel_id=1, source_target_pairs={{0,8},{8,16},{16,24},{24,32},{32,40},{40,48},{48,56},{56,64},{64,7... | collective-permute-start | bytes 196616 | tf_op jit(solution)/shard_map/ppermute | solution.py:350
